TPU v7x, 256 devices: a whole 4x4x8 slice. The times are simulated.
256 devices in a mesh: row: 32 (over x_hi, z, core), col: 8 (over x_lo, y).
Axes of the slice: x: 4 (x_hi: 2, x_lo: 2; x = x_hi * 2 + x_lo), y: 4, z: 8, core: 2. Of those that a mesh axis runs over, the one named last changes fastest.
Arguments:
- seqs: int32 [128, 4096], replicated, may hold values from 0 to 3
- fields: float32 [16384], replicated, may hold values from -4 to 320
- band: float32 [16384, 8704], P('row', 'col'), may hold values from -0.125 to 0.125, as said below
Outputs:
- new_band: float32 [16384, 8704], P('row', 'col')
- new_fields: float32 [16384], P(('row', 'col'))
Inputs may be any that keep to these rules, and one draw needn't show every extreme that they name: band entries that are not live are zero, the tiles with j = 0 are symmetric, and entries whose row and column states belong to the same locus are zero.
All inputs are finite; a program needn't handle non-finite values.
Results may differ from a plain program's by a relative error of at most 0.0003.
Values sent between devices are 32-bit elements; how exact they have to be, the bound alone decides.
No kernel may reach another device: no remote copies, remote signals or barrier semaphores. Data moves between devices by JAX's collectives and lax.ppermute only.
A program may use at most 64 MiB of HBM per device.

v0:
```python
import jax
import jax.numpy as jnp
from jax import lax
from jax.sharding import PartitionSpec as P

Q = 4


step_rate = 1.0
coupling_decay = 0.25
field_decay = 0.1


def onehot_of(state_codes):
    table = state_codes[:, :, None] == jnp.arange(Q, dtype=jnp.int32)[None, None, :]
    return table.astype(jnp.float32).reshape(state_codes.shape[0], -1)


def residual_of(logits, onehot_part):
    batch_size = logits.shape[0]
    grouped = logits.reshape(batch_size, -1, Q)
    highest = jnp.max(grouped, axis=2, keepdims=True)
    expon = jnp.exp(grouped - highest)
    probabilities = expon / jnp.sum(expon, axis=2, keepdims=True)
    return onehot_part - probabilities.reshape(batch_size, -1)


def shards(seqs, fields, band):
    batch_size = seqs.shape[0]
    row_span, local_width = band.shape
    row_count = lax.axis_size("row")
    col_count = lax.axis_size("col")
    piece = row_span // col_count
    tile_count = local_width // piece
    half_count = row_count // 2
    row_at = lax.axis_index("row")
    col_at = lax.axis_index("col")
    row_start = row_at * row_span
    share_start = row_start + col_at * piece
    slot_ids = jnp.arange(tile_count, dtype=jnp.int32)
    col_starts = (row_at + slot_ids) % row_count * row_span + col_at * piece
    col_states = (col_starts[:, None] + jnp.arange(piece, dtype=jnp.int32)[None, :]).reshape(-1)
    locus_ids = (
        col_starts[:, None] // Q + jnp.arange(piece // Q, dtype=jnp.int32)[None, :]
    ).reshape(-1)
    onehot_cols = onehot_of(jnp.take(seqs, locus_ids, axis=1))
    onehot_rows = onehot_of(lax.dynamic_slice_in_dim(seqs, row_start // Q, row_span // Q, 1))
    slot_of_col = jnp.arange(local_width, dtype=jnp.int32) // piece
    live = jnp.where((slot_of_col == half_count) & (row_at >= half_count), 0.0, 1.0).astype(
        jnp.float32
    )
    routed = live * (slot_of_col > 0).astype(jnp.float32)
    row_part = lax.dot_general(
        onehot_cols * live[None, :],
        band,
        (((1,), (1,)), ((), ())),
        precision=lax.Precision.HIGHEST,
        preferred_element_type=jnp.float32,
    )
    col_part = (
        jnp.dot(
            onehot_rows, band, precision=lax.Precision.HIGHEST, preferred_element_type=jnp.float32
        )
        * routed[None, :]
    )
    col_pieces = col_part.reshape(batch_size, tile_count, piece)
    padded = jnp.concatenate(
        [col_pieces, jnp.zeros((batch_size, row_count - tile_count, piece), jnp.float32)], axis=1
    )
    placed = jnp.roll(padded, row_at, axis=1)
    col_hot = (jnp.arange(col_count, dtype=jnp.int32) == col_at).astype(jnp.float32)
    row_hot = (jnp.arange(row_count, dtype=jnp.int32) == row_at).astype(jnp.float32)
    dense = placed[:, :, None, :] * col_hot[None, None, :, None]
    dense = dense + row_part.reshape(batch_size, 1, col_count, piece) * row_hot[None, :, None, None]
    share = lax.psum_scatter(
        dense.reshape(batch_size, -1), ("row", "col"), scatter_dimension=1, tiled=True
    )
    fields_share = lax.dynamic_slice_in_dim(fields, share_start, piece, 0)
    onehot_share = onehot_of(lax.dynamic_slice_in_dim(seqs, share_start // Q, piece // Q, 1))
    resid_share = residual_of(share + fields_share[None, :], onehot_share)
    resid_all = lax.all_gather(resid_share, ("row", "col"), axis=1, tiled=True)
    resid_rows = lax.dynamic_slice_in_dim(resid_all, row_start, row_span, 1)
    piece_rows = lax.dynamic_index_in_dim(
        resid_all.reshape(batch_size, row_count, col_count, piece), col_at, 2, keepdims=False
    )
    resid_cols = jnp.roll(piece_rows, -row_at, axis=1)[:, :tile_count].reshape(batch_size, -1)
    gradient = lax.dot_general(
        resid_rows,
        onehot_cols,
        (((0,), (0,)), ((), ())),
        precision=lax.Precision.HIGHEST,
        preferred_element_type=jnp.float32,
    )
    gradient = gradient + lax.dot_general(
        onehot_rows,
        resid_cols,
        (((0,), (0,)), ((), ())),
        precision=lax.Precision.HIGHEST,
        preferred_element_type=jnp.float32,
    )
    row_locus = (row_start + jnp.arange(row_span, dtype=jnp.int32)) // Q
    col_locus = col_states // Q
    keep_mask = live[None, :] * (row_locus[:, None] != col_locus[None, :]).astype(jnp.float32)
    new_band = live[None, :] * (
        band + step_rate * (keep_mask * (gradient / batch_size) - coupling_decay * band)
    )
    new_fields = fields_share + step_rate * (
        jnp.sum(resid_share, axis=0) / batch_size - field_decay * fields_share
    )
    return (new_band, new_fields)


def solution(mesh):
    in_specs = (P(), P(), P("row", "col"))
    out_specs = (P("row", "col"), P(("row", "col")))
    return jax.shard_map(shards, mesh=mesh, in_specs=in_specs, out_specs=out_specs, check_vma=False)
```

profile of v0, /device:TPU:1, one launch (start us, length us, event | category | flops | bytes accessed | tf_op | source)
XLA Modules:
  0.0 2044.3 jit_solution(12314321634719738828)
XLA Ops:
  7.3 0.1 add.222
  7.6 3.0 copy.15
  10.6 0.1 mul.127
  10.7 0.1 mul.128
  10.8 0.1 copy.16
  11.0 2.0 copy.17
  13.0 0.1 mul.119
  13.1 1.0 constant_dynamic-slice_fusion
  14.1 0.1 copy.14
  14.3 0.1 eq.138
  14.4 2.6 gather_fusion
  17.0 0.1 select_bitcast_fusion
  17.1 0.4 fusion.9
  17.5 3.7 fusion.43
  21.3 1.2 convolution_multiply_fusion
  22.5 0.1 concatenate.6
  22.6 0.3 fusion.7
  22.9 7.1 fusion.1
  30.1 1.0 constant_dynamic-slice_fusion.1
  31.1 0.1 eq.132
  31.3 0.8 dynamic_slice.21
  32.0 1270.7 %reduce-scatter.2.cloned.1.call-done = f32[128,64]{0,1:T(8,128)} async-done(((f32[128,16384]{0,1:T(8,128)}), f32[128,64]{0,1:T(8,128)}) %reduce-scatter.2.cloned.1.call-update) | async-done | bytes 32784 | tf_op jit(solution)/shard_map/reduce_scatter | solution.py:75
  1302.7 0.8 broadcast_add_fusion
  1303.6 1.6 fusion.41
  1305.3 0.1 eq.152
  1305.7 1.3 subtract_add_fusion
  1307.0 723.9 %all-gather.2.cloned.1.call-done = f32[128,16384]{0,1:T(8,128)} async-done(((f32[128,64]{0,1:T(8,128)}), f32[128,16384]{0,1:T(8,128)}) %all-gather.2.cloned.1.call-update) | async-done | bytes 8388624 | tf_op jit(solution)/shard_map/all_gather | solution.py:81
  2030.9 1.3 dynamic-slice_bitcast_fusion
  2032.2 0.1 fusion.8
  2032.4 0.1 eq.143
  2032.5 2.0 fusion.10
  2034.5 2.9 fusion.6
  (32 shorter events, 0.9 us)
Async XLA Ops:
  7.2 1295.6 %reduce-scatter.2.cloned.1.call-start = ((), (), s32[]{:S(2)}) async-start(), calls=%async_computation.1 | async-start | bytes 8421376 | tf_op jit(solution)/shard_map/reduce_scatter | solution.py:75
  7.5 3.4 copy-start
  30.0 2000.9 %all-gather.2.cloned.1.call-start = ((), (), s32[]{:S(2)}) async-start(), calls=%async_computation.2 | async-start | bytes 8421376 | tf_op jit(solution)/shard_map/all_gather | solution.py:81
Sparse Core Ops, SparseCore 0:
  30.1 1272.5 reduce-scatter.1
  1305.4 725.4 all-gather.1
where the time goes:
time: 2050 us; the launch traced here: 2040 us
  waiting for transfers between devices  1990 us (97%)
    reduce_scatter x1, waiting for transfers between devices, shards(): lax.psum_scatter(dense.reshape(batch_size, -1), ('row', 'col'), scatter_d...  1270 us
    all_gather x1, waiting for transfers between devices, shards(): resid_all = lax.all_gather(resid_share, ('row', 'col'), axis=1, tiled=True)  724 us
  transfers between devices with their start and end apart: 2, of which 2 were waited for; matrix products, arithmetic and copies ran while one was open for 0% of the time, Pallas kernels for 0%

commit v1 on v0

v1 whole, which is shorter than its diff:
```python
import jax
import jax.numpy as jnp
from jax import lax
from jax.experimental import pallas as pl
from jax.experimental.pallas import tpu as pltpu
from jax.sharding import PartitionSpec as P

Q = 4
ROWS = 32
COLS = 8
HALF = 16
TILES = 17
PIECE = 64
LOCI = 16
SPAN = 512
BAND = TILES * PIECE
BATCH = 128
SENT = 3 * LOCI

step_rate = 1.0
coupling_decay = 0.25
field_decay = 0.1

LOW_GROUPS = [[h * HALF + l for l in range(HALF)] for h in range(2)]
SWAP_HALVES = [(i, i ^ HALF) for i in range(ROWS)]

f32 = jnp.float32
bf16 = jnp.bfloat16
NT = (((1,), (1,)), ((), ()))


def iota(shape, dim):
    return lax.broadcasted_iota(jnp.int32, shape, dim)


def split(x):
    hi = x.astype(bf16)
    return hi, (x - hi.astype(f32)).astype(bf16)


def mm(a, b):
    return jnp.dot(a, b, preferred_element_type=f32)


def seq_block(seqs_ref, at):
    start = pl.multiple_of(at * BATCH, BATCH)
    return seqs_ref[:, pl.ds(start, BATCH)].astype(f32).astype(bf16)


def logits_kernel(seqs_ref, band_ref, col_ref, last_ref, row_ref, codes_ref, hot, row_t, col_t):
    row_at = lax.axis_index("row")
    col_at = lax.axis_index("col")
    low_at = lax.rem(row_at, HALF)
    lane = iota((BATCH, 128), 1)
    pick = (iota((128, 128), 0) == col_at * LOCI + lane % PIECE // Q).astype(f32).astype(bf16)
    pick_loci = (
        (iota((LOCI, 128), 1) == col_at * LOCI + iota((LOCI, 128), 0)).astype(f32).astype(bf16)
    )
    spread = (iota((SPAN, 128), 1) == iota((SPAN, 128), 0) // Q).astype(f32).astype(bf16)
    state = (lane % Q).astype(f32)
    dead = row_at >= HALF
    own = None
    for pair in range(9):
        left = seq_block(seqs_ref, lax.rem(row_at + 2 * pair, ROWS))
        codes = mm(left, pick)
        if pair == 0:
            own = left
            codes_ref[0] = lax.dot_general(pick_loci, left, NT, preferred_element_type=f32)
        if pair < 8:
            right = seq_block(seqs_ref, lax.rem(row_at + 2 * pair + 1, ROWS))
            codes = jnp.where(lane < PIECE, codes, mm(right, pick))
        else:
            codes_ref[1] = lax.dot_general(pick_loci, left, NT, preferred_element_type=f32)
            codes = jnp.where((lane < PIECE) & jnp.logical_not(dead), codes, -1.0)
        hot[:, pair * 128 : pair * 128 + 128] = (codes == state).astype(f32).astype(bf16)
    codes_rows = lax.dot_general(spread, own, NT, preferred_element_type=f32)
    hot_rows = (codes_rows == (iota((SPAN, 128), 0) % Q).astype(f32)).astype(f32).astype(bf16)
    hi, lo = split(band_ref[...])
    col_t[...] = mm(hi, hot_rows) + mm(lo, hot_rows)
    part = mm(hot[:, :BAND], hi) + mm(hot[:, :BAND], lo)
    row_t[...] = part.T
    last = col_t[pl.ds(3, TILES * LOCI, stride=Q), :]
    last_row = row_t[pl.ds(3, COLS * LOCI, stride=Q), :]
    for a in range(3):
        diff = col_t[pl.ds(a, TILES * LOCI, stride=Q), :] - last
        place = slice(a * LOCI, (a + 1) * LOCI)
        col_ref[low_at, place, :] = jnp.zeros((LOCI, BATCH), f32)
        for j in range(1, HALF):
            to = lax.rem(low_at + j, HALF)
            col_ref[to, place, :] = diff[j * LOCI : (j + 1) * LOCI]
        last_ref[place, :] = jnp.where(dead, 0.0, diff[HALF * LOCI :])
        diff_row = row_t[pl.ds(a, COLS * LOCI, stride=Q), :] - last_row
        for c in range(COLS):
            row_ref[c, place, :] = diff_row[c * LOCI : (c + 1) * LOCI]


def hot_kernel(seqs_ref, hot_cols_ref, hot_rows_ref):
    row_at = lax.axis_index("row")
    col_at = lax.axis_index("col")
    pick = (
        (iota((PIECE, 128), 1) == col_at * LOCI + iota((PIECE, 128), 0) // Q)
        .astype(f32)
        .astype(bf16)
    )
    state = (iota((PIECE, 128), 0) % Q).astype(f32)
    for j in range(TILES):
        block = seq_block(seqs_ref, lax.rem(row_at + j, ROWS))
        codes = lax.dot_general(pick, block, NT, preferred_element_type=f32)
        hot_cols_ref[j * PIECE : (j + 1) * PIECE, :] = (codes == state).astype(f32).astype(bf16)
    own = seq_block(seqs_ref, row_at)
    spread = (iota((128, SPAN), 0) == iota((128, SPAN), 1) // Q).astype(f32).astype(bf16)
    codes = mm(own, spread)
    hot_rows_ref[...] = (
        (codes == (iota((BATCH, SPAN), 1) % Q).astype(f32)).astype(f32).astype(bf16)
    )


def sum_kernel(col_ref, last_ref, row_ref, out_ref):
    low_at = lax.rem(lax.axis_index("row"), HALF)
    own = row_ref[0]
    for c in range(1, COLS):
        own = own + row_ref[c]
    other = last_ref[...]
    for s in range(HALF):
        part = col_ref[s]
        own = own + jnp.where(s <= low_at, part, 0.0)
        other = other + jnp.where(s > low_at, part, 0.0)
    out_ref[:SENT, :] = own
    out_ref[SENT:, :] = other


def softmax_kernel(
    here_ref, there_ref, codes_ref, fields_ref, low_ref, row_ref, other_ref, new_fields_ref
):
    row_at = lax.axis_index("row")
    col_at = lax.axis_index("col")
    low_at = lax.rem(row_at, HALF)
    lane = iota((LOCI, 128), 1)
    locus = iota((LOCI, 128), 0)
    start = col_at % 2 * PIECE
    own = []
    other = []
    columns = []
    for block in range(2):
        block_at = lax.rem(row_at + block * HALF, ROWS)
        line = fields_ref[pl.ds(block_at * 4 + col_at // 2, 1), :]
        columns = [
            jnp.sum(jnp.where(lane == start + locus * Q + a, line, 0.0), axis=1, keepdims=True)
            for a in range(Q)
        ]
        if block == 0:
            own_columns = columns
        diffs = []
        for a in range(3):
            here = here_ref[block * SENT + a * LOCI : block * SENT + (a + 1) * LOCI, :]
            flip = (1 - block) * SENT + a * LOCI
            there = there_ref[flip : flip + LOCI, :]
            diffs.append(here + there + (columns[a] - columns[3]))
        highest = jnp.maximum(jnp.maximum(diffs[0], diffs[1]), jnp.maximum(diffs[2], 0.0))
        expon = [jnp.exp(d - highest) for d in diffs]
        total = expon[0] + expon[1] + expon[2] + jnp.exp(-highest)
        codes = codes_ref[block]
        resid = [
            jnp.where(codes == float(a), 1.0, 0.0) - expon[a] / total for a in range(3)
        ]
        if block == 0:
            own = resid
        else:
            other = resid
    sums = [jnp.sum(x, axis=1, keepdims=True) for x in own]
    sums.append(-(sums[0] + sums[1] + sums[2]))
    line = jnp.zeros((LOCI, 128), f32)
    for a in range(Q):
        value = own_columns[a] + step_rate * (sums[a] / BATCH - field_decay * own_columns[a])
        line = line + jnp.where(lane == locus * Q + a, value, 0.0)
    new_fields_ref[...] = jnp.sum(line, axis=0, keepdims=True)
    for a in range(3):
        place = slice(a * LOCI, (a + 1) * LOCI)
        other_ref[place, :] = other[a]
        for c in range(COLS):
            row_ref[c, place, :] = own[a]
        for s in range(HALF):
            low_ref[s, place, :] = jnp.where(low_at >= s, own[a], other[a])


def update_kernel(
    band_ref, low_ref, other_ref, row_ref, hot_cols_ref, hot_rows_ref, out_ref, rows, cols
):
    row_at = lax.axis_index("row")
    col_at = lax.axis_index("col")
    low_at = lax.rem(row_at, HALF)
    for j in range(TILES):
        if j < HALF:
            part = low_ref[lax.rem(low_at + j, HALF)]
        else:
            part = other_ref[...]
        pieces = [part[a * LOCI : (a + 1) * LOCI] for a in range(3)]
        pieces.append(-(pieces[0] + pieces[1] + pieces[2]))
        for a in range(Q):
            cols[pl.ds(j * PIECE + a, LOCI, stride=Q), :] = pieces[a]
    for c in range(COLS):
        pieces = [row_ref[c, a * LOCI : (a + 1) * LOCI, :] for a in range(3)]
        pieces.append(-(pieces[0] + pieces[1] + pieces[2]))
        for a in range(Q):
            rows[pl.ds(c * PIECE + a, LOCI, stride=Q), :] = pieces[a]
    rows_hi, rows_lo = split(rows[...].T)
    right = jnp.concatenate([rows_hi, rows_lo, hot_rows_ref[...], hot_rows_ref[...]], axis=0)
    dead = row_at >= HALF
    for chunk in range(4):
        at = slice(chunk * 272, (chunk + 1) * 272)
        cols_hi, cols_lo = split(cols[at, :])
        hot = hot_cols_ref[at, :]
        gradient = mm(jnp.concatenate([hot, hot, cols_hi, cols_lo], axis=1), right)
        band = band_ref[at, :]
        spot = iota((272, SPAN), 0) + chunk * 272
        if chunk == 0:
            same = (spot < PIECE) & (
                (col_at * PIECE + spot) // Q == iota((272, SPAN), 1) // Q
            )
            gradient = jnp.where(same, 0.0, gradient)
        new = band + step_rate * (gradient / BATCH - coupling_decay * band)
        if chunk == 3:
            new = jnp.where(dead & (spot >= HALF * PIECE), 0.0, new)
        out_ref[at, :] = new


def call(kernel, outs, scratch=(), name=None):
    return pl.pallas_call(
        kernel,
        out_shape=outs,
        scratch_shapes=list(scratch),
        compiler_params=pltpu.CompilerParams(vmem_limit_bytes=48 * 1024 * 1024),
        name=name,
    )


def arr(*shape, dtype=f32):
    return jax.ShapeDtypeStruct(shape, dtype)


def shards(seqs, fields, band):
    band_t = band.T
    col_send, last, row_send, codes = call(
        logits_kernel,
        (
            arr(HALF, SENT, BATCH),
            arr(SENT, BATCH),
            arr(COLS, SENT, BATCH),
            arr(2, LOCI, BATCH),
        ),
        [
            pltpu.VMEM((BATCH, 9 * 128), bf16),
            pltpu.VMEM((SPAN, BATCH), f32),
            pltpu.VMEM((BAND, BATCH), f32),
        ],
        "logit_parts",
    )(seqs, band_t)
    row_got = lax.all_to_all(row_send, "col", 0, 0, tiled=True)
    col_got = lax.all_to_all(col_send, "row", 0, 0, tiled=True, axis_index_groups=LOW_GROUPS)
    hot_cols, hot_rows = call(
        hot_kernel, (arr(BAND, BATCH, dtype=bf16), arr(BATCH, SPAN, dtype=bf16)), name="one_hots"
    )(seqs)
    here = call(sum_kernel, arr(2 * SENT, BATCH), name="sum_parts")(col_got, last, row_got)
    there = lax.ppermute(here, "row", SWAP_HALVES)
    low_send, row_resid, other, new_fields = call(
        softmax_kernel,
        (
            arr(HALF, SENT, BATCH),
            arr(COLS, SENT, BATCH),
            arr(SENT, BATCH),
            arr(1, 128),
        ),
        name="softmax",
    )(here, there, codes, fields.reshape(-1, 128))
    row_all = lax.all_to_all(row_resid, "col", 0, 0, tiled=True)
    low_all = lax.all_to_all(low_send, "row", 0, 0, tiled=True, axis_index_groups=LOW_GROUPS)
    new_band_t = call(
        update_kernel,
        arr(BAND, SPAN),
        [pltpu.VMEM((SPAN, BATCH), f32), pltpu.VMEM((BAND, BATCH), f32)],
        "update",
    )(band_t, low_all, other, row_all, hot_cols, hot_rows)
    return new_band_t.T, new_fields[0, :PIECE]


def solution(mesh):
    in_specs = (P(), P(), P("row", "col"))
    out_specs = (P("row", "col"), P(("row", "col")))
    return jax.shard_map(shards, mesh=mesh, in_specs=in_specs, out_specs=out_specs, check_vma=False)
```

time: 2050 us -> 78.1 us (0.04)
  waiting for transfers between devices: 1990 us -> 14.1 us
  blocking collectives: 0 us -> 44.7 us
    reduce_scatter x1 -> x0, waiting for transfers between devices: 1270 us -> none  [shards(): lax.psum_scatter(dense.reshape(batch_size, -1), ('row', 'col'), scatter_d...]
    all_gather x1 -> x0, waiting for transfers between devices: 724 us -> none  [shards(): resid_all = lax.all_gather(resid_share, ('row', 'col'), axis=1, tiled=True)]
    all_to_all x0 -> x3, blocking collectives: none -> 44.7 us  [the longest x1 24.8 us: shards(): lax.all_to_all(col_send, 'row', 0, 0, tiled=True, axis_index_groups=LOW_G...]
  transfers between devices with their start and end apart: 2 -> 2, of which waited for: 2 -> 2; matrix products, arithmetic and copies ran while one was open for 0% -> 1% of each run, Pallas kernels for 0% -> 1%
where the time goes in v1:
time: 78.1 us; the launch traced here: 77.7 us
  blocking collectives  44.7 us (57%)
  waiting for transfers between devices  14.1 us (18%)
  starting transfers between devices  7.52 us (10%)
  Pallas kernels  5.37 us (7%)
  local copies, waits for them, and re-layouts  5.32 us (7%)
    all_to_all x1, blocking collectives, shards(): lax.all_to_all(col_send, 'row', 0, 0, tiled=True, axis_index_groups=LOW_G...  24.8 us
    all_to_all x1, waiting for transfers between devices, shards(): lax.all_to_all(low_send, 'row', 0, 0, tiled=True, axis_index_groups=LOW_G...  11.9 us
    all_to_all x1, blocking collectives, shards(): row_got = lax.all_to_all(row_send, 'col', 0, 0, tiled=True)  11.6 us
    all_to_all x1, blocking collectives, shards(): row_all = lax.all_to_all(row_resid, 'col', 0, 0, tiled=True)  8.27 us
    all_to_all x1, starting transfers between devices, shards(): lax.all_to_all(low_send, 'row', 0, 0, tiled=True, axis_index_groups=LOW_G...  4.98 us
    unnamed x10, local copies, waits for them, and re-layouts  4.81 us
    ppermute x1, starting transfers between devices, shards(): there = lax.ppermute(here, 'row', SWAP_HALVES)  2.53 us
    pallas_call x1, Pallas kernels, shards(): call(update_kernel, arr(BAND, SPAN), [pltpu.VMEM((SPAN, BATCH), f32), plt...  2.3 us
  transfers between devices with their start and end apart: 2, of which 2 were waited for; matrix products, arithmetic and copies ran while one was open for 1% of the time, Pallas kernels for 1%

profile of v1, /device:TPU:1, one launch (start us, length us, event | category | flops | bytes accessed | tf_op | source)
XLA Modules:
  0.0 77.7 jit_solution(1816194948588625389)
XLA Ops:
  0.6 0.0 copy-start
  0.6 1.6 %copy-done = f32[512,1088]{0,1:T(8,128)S(1)} copy-done((f32[512,1088]{0,1:T(8,128)S(1)}, f32[512,1088]{0,1:T(8,128)}, u32[]{:S(2)}) %copy-start) | copy-done | bytes 2228248
  2.3 0.0 copy-start.2
  2.3 1.6 %copy-done.2 = s32[128,4096]{1,0:T(8,128)S(1)} copy-done((s32[128,4096]{1,0:T(8,128)S(1)}, s32[128,4096]{1,0:T(8,128)}, u32[]{:S(2)}) %copy-start.2) | copy-done | bytes 2097176
  3.9 0.0 copy-start.4
  3.9 1.5 %logit_parts.1 = (f32[16,48,128]{2,1,0:T(8,128)S(1)}, f32[48,128]{1,0:T(8,128)S(1)}, f32[8,48,128]{2,1,0:T(8,128)S(1)}, f32[2,16,128]{2,1,0:T(8,128)S(1)}) custom-call(s32[128,4096]{1,0:T(8,128)S(1)} %copy-done.2, f32[1088,512]{1,0:T(8,128)S(1)} %bitcast.5), custom_call_target="tpu_custom_call" | custom-call | tf_op jit(solution)/shard_map/logit_parts/pallas_call | solution.py:243
  5.4 11.6 %all_to_all.20.row_ref = f32[8,48,128]{2,1,0:T(8,128)S(1)} all-to-all(f32[8,48,128]{2,1,0:T(8,128)S(1)} %get-tuple-element.14), channel_id=1, replica_groups=mesh['row'=32,'col'=8] {'col'}, dimensions={0} | all-to-all | bytes 393216 | tf_op jit(solution)/shard_map/all_to_all | solution.py:258
  17.0 24.8 %all_to_all.21.col_ref = f32[16,48,128]{2,1,0:T(8,128)S(1)} all-to-all(f32[16,48,128]{2,1,0:T(8,128)S(1)} %get-tuple-element.12), channel_id=1, replica_groups={{0,8,16,24,32,40,48,56,64,72,80,88,96,104,112,120},{128,136,144,152,160..., dimensions={0} | all-to-all | bytes 786432 | tf_op jit(solution)/shard_map/all_to_all | solution.py:259
  41.8 0.0 copy-start.1
  41.8 0.1 sum_parts.1.here_ref
  41.9 2.5 %collective-permute-start = (f32[96,128]{1,0:T(8,128)S(1)}, f32[96,128]{1,0:T(8,128)S(1)}, u32[]{:S(2)}, u32[]{:S(2)}) collective-permute-start(f32[96,128]{1,0:T(8,128)S(1)} %sum_parts.1.here_ref), channel_id=1, source_target_pairs={{0,128},{8,136},{16,144},{24,152},{32,160},{40,168},{48,176},{56,1... | collective-permute-start | bytes 147464 | tf_op jit(solution)/shard_map/ppermute | solution.py:264
  44.5 2.2 %collective-permute-done.there_ref = f32[96,128]{1,0:T(8,128)S(1)} collective-permute-done((f32[96,128]{1,0:T(8,128)S(1)}, f32[96,128]{1,0:T(8,128)S(1)}, u32[]{:S(2)}, u32[]{:S(2)}) %collective-permute-start) | collective-permute-done | bytes 49184 | tf_op jit(solution)/shard_map/ppermute | solution.py:264
  46.7 0.0 copy-done.4
  46.7 0.9 %softmax.1 = (f32[16,48,128]{2,1,0:T(8,128)}, f32[8,48,128]{2,1,0:T(8,128)S(1)}, f32[48,128]{1,0:T(8,128)S(1)}, f32[1,128]{1,0:T(1,128)S(1)}) custom-call(f32[96,128]{1,0:T(8,128)S(1)} %sum_parts.1.here_ref, f32[96,128]{1,0:T(8,128)S(1)} %collective-permute-done.there_ref, f32[2,16,128]{2,1,0:T(8,128)S(1)} %get-tuple-element.15.codes_ref, f32[128,128]{1,0:T(8,128)S(1)} %bitcast.7), custom_call_target="tpu_custom_call" | custom-call | tf_op jit(solution)/shard_map/softmax/pallas_call | solution.py:265
  47.6 8.3 %all_to_all.22.row_ref = f32[8,48,128]{2,1,0:T(8,128)S(1)} all-to-all(f32[8,48,128]{2,1,0:T(8,128)S(1)} %get-tuple-element.18), channel_id=1, replica_groups=mesh['row'=32,'col'=8] {'col'}, dimensions={0} | all-to-all | bytes 393216 | tf_op jit(solution)/shard_map/all_to_all | solution.py:275
  55.9 5.0 %all-to-all-start.2 = ((f32[16,48,128]{2,1,0:T(8,128)}), f32[16,48,128]{2,1,0:T(8,128)S(1)}, u32[]{:S(2)}, u32[]{:S(2)}) async-start(f32[16,48,128]{2,1,0:T(8,128)} %get-tuple-element.16), calls=%async_computation.2 | async-start | bytes 786432 | tf_op jit(solution)/shard_map/all_to_all | solution.py:276
  60.8 0.0 copy-start.3
  60.9 1.6 %copy-done.3 = s32[128,4096]{1,0:T(8,128)S(1)} copy-done((s32[128,4096]{1,0:T(8,128)S(1)}, s32[128,4096]{1,0:T(8,128)}, u32[]{:S(2)}) %copy-start.3) | copy-done | bytes 2097176
  62.4 0.5 one_hots.1
  63.0 0.5 slice_bitcast_fusion
  63.5 11.9 %all-to-all-done.2.low_ref = f32[16,48,128]{2,1,0:T(8,128)S(1)} async-done(((f32[16,48,128]{2,1,0:T(8,128)}), f32[16,48,128]{2,1,0:T(8,128)S(1)}, u32[]{:S(2)}, u32[]{:S(2)}) %all-to-all-start.2) | async-done | bytes 393248 | tf_op jit(solution)/shard_map/all_to_all | solution.py:276
  75.4 0.0 copy-done.1
  75.4 2.3 %update.1 = f32[1088,512]{1,0:T(8,128)} custom-call(f32[1088,512]{1,0:T(8,128)S(1)} %bitcast.6, f32[16,48,128]{2,1,0:T(8,128)S(1)} %all-to-all-done.2.low_ref, f32[48,128]{1,0:T(8,128)S(1)} %get-tuple-element.17.other_ref, f32[8,48,128]{2,1,0:T(8,128)S(1)} %all_to_all.22.row_ref, bf16[1088,128]{1,0:T(8,128)(2,1)S(1)} %get-tuple-element.19.hot_cols_ref, ...), custom_call_target="tpu_custom_call" | custom-call | tf_op jit(solution)/shard_map/update/pallas_call | solution.py:277
Async XLA Ops:
  0.6 1.6 %copy-start = (f32[512,1088]{0,1:T(8,128)S(1)}, f32[512,1088]{0,1:T(8,128)}, u32[]{:S(2)}) copy-start(f32[512,1088]{0,1:T(8,128)} %param.5) | copy-start | bytes 6684676
  2.3 1.6 %copy-start.2 = (s32[128,4096]{1,0:T(8,128)S(1)}, s32[128,4096]{1,0:T(8,128)}, u32[]{:S(2)}) copy-start(s32[128,4096]{1,0:T(8,128)} %seqs_ref.3) | copy-start | bytes 6291460
  3.9 42.8 %copy-start.4 = (f32[16384]{0:T(1024)S(1)}, f32[16384]{0:T(1024)}, u32[]{:S(2)}) copy-start(f32[16384]{0:T(1024)} %param.4) | copy-start | bytes 196612
  41.8 33.6 %copy-start.1 = (f32[512,1088]{0,1:T(8,128)S(1)}, f32[512,1088]{0,1:T(8,128)}, u32[]{:S(2)}) copy-start(f32[512,1088]{0,1:T(8,128)} %param.5) | copy-start | bytes 6684676
  41.9 4.8 %collective-permute-start = (f32[96,128]{1,0:T(8,128)S(1)}, f32[96,128]{1,0:T(8,128)S(1)}, u32[]{:S(2)}, u32[]{:S(2)}) collective-permute-start(f32[96,128]{1,0:T(8,128)S(1)} %sum_parts.1.here_ref), channel_id=1, source_target_pairs={{0,128},{8,136},{16,144},{24,152},{32,160},{40,168},{48,176},{56,1... | collective-permute-start | bytes 147464 | tf_op jit(solution)/shard_map/ppermute | solution.py:264
  55.9 19.5 %all-to-all-start.2 = ((f32[16,48,128]{2,1,0:T(8,128)}), f32[16,48,128]{2,1,0:T(8,128)S(1)}, u32[]{:S(2)}, u32[]{:S(2)}) async-start(f32[16,48,128]{2,1,0:T(8,128)} %get-tuple-element.16), calls=%async_computation.2 | async-start | bytes 786432 | tf_op jit(solution)/shard_map/all_to_all | solution.py:276
  60.8 1.6 %copy-start.3 = (s32[128,4096]{1,0:T(8,128)S(1)}, s32[128,4096]{1,0:T(8,128)}, u32[]{:S(2)}) copy-start(s32[128,4096]{1,0:T(8,128)} %seqs_ref.3) | copy-start | bytes 6291460

commit v2 on v1

v2 whole, which is shorter than its diff:
```python
import jax
import jax.numpy as jnp
from jax import lax
from jax.experimental import pallas as pl
from jax.experimental.pallas import tpu as pltpu
from jax.sharding import PartitionSpec as P

Q = 4
ROWS = 32
COLS = 8
HALF = 16
TILES = 17
PIECE = 64
LOCI = 16
SPAN = 512
BAND = TILES * PIECE
BATCH = 128
SENT = 3 * LOCI

step_rate = 1.0
coupling_decay = 0.25
field_decay = 0.1

DEPTH = 8
Z_GROUPS = [[(h * DEPTH + z) * 2 + k for z in range(DEPTH)] for h in range(2) for k in range(2)]
SWAP_CORES = [(i, i ^ 1) for i in range(ROWS)]
SWAP_HALVES = [(i, i ^ HALF) for i in range(ROWS)]


def swap_cols(x, step):
    return lax.ppermute(x, "col", [(i, i ^ step) for i in range(COLS)])


NEAR = 4
CHUNKS = [slice(0, 256), slice(256, 512), slice(512, 768), slice(768, BAND)]

f32 = jnp.float32
bf16 = jnp.bfloat16
NT = (((1,), (1,)), ((), ()))


def iota(shape, dim):
    return lax.broadcasted_iota(jnp.int32, shape, dim)


def split(x):
    hi = x.astype(bf16)
    return hi, (x - hi.astype(f32)).astype(bf16)


def mm(a, b):
    return jnp.dot(a, b, preferred_element_type=f32)


def logits_kernel(
    seqs_ref,
    band_ref,
    codes_ref,
    mine_ref,
    core_ref,
    keep_ref,
    give_ref,
    hot,
    hot_rows_ref,
    blocks,
    band,
    row_t,
    col_t,
    block_sems,
    band_sems,
):
    row_at = lax.axis_index("row")
    col_at = lax.axis_index("col")
    block_copies = []
    for j in range(TILES):
        start = pl.multiple_of(lax.rem(row_at + j, ROWS) * BATCH, BATCH)
        block_copies.append(
            pltpu.make_async_copy(
                seqs_ref.at[:, pl.ds(start, BATCH)], blocks.at[j], block_sems.at[j]
            )
        )
    band_copies = [
        pltpu.make_async_copy(band_ref.at[at], band.at[at], band_sems.at[i])
        for i, at in enumerate(CHUNKS)
    ]
    for copy in block_copies + band_copies:
        copy.start()
    lane = iota((BATCH, 128), 1)
    pick = (iota((128, 128), 0) == col_at * LOCI + lane % PIECE // Q).astype(f32).astype(bf16)
    pick_loci = (
        (iota((LOCI, 128), 1) == col_at * LOCI + iota((LOCI, 128), 0)).astype(f32).astype(bf16)
    )
    spread = (iota((SPAN, 128), 1) == iota((SPAN, 128), 0) // Q).astype(f32).astype(bf16)
    state = (lane % Q).astype(f32)
    dead = row_at >= HALF

    for copy in block_copies:
        copy.wait()

    def block(j):
        return blocks[j].astype(f32).astype(bf16)

    own = block(0)
    codes_ref[0] = lax.dot_general(pick_loci, own, NT, preferred_element_type=f32)
    codes_rows = lax.dot_general(spread, own, NT, preferred_element_type=f32)
    hot_rows = (codes_rows == (iota((SPAN, 128), 0) % Q).astype(f32)).astype(f32).astype(bf16)
    hot_rows_ref[...] = hot_rows
    for pair in range(9):
        left = block(2 * pair) if pair else own
        codes = mm(left, pick)
        if pair < 8:
            codes = jnp.where(lane < PIECE, codes, mm(block(2 * pair + 1), pick))
        else:
            codes_ref[1] = lax.dot_general(pick_loci, left, NT, preferred_element_type=f32)
            codes = jnp.where((lane < PIECE) & jnp.logical_not(dead), codes, -1.0)
        hot[:, pair * 128 : pair * 128 + 128] = (codes == state).astype(f32).astype(bf16)
    part = None
    for chunk, at in enumerate(CHUNKS):
        if chunk % 2 == 0:
            band_copies[chunk].wait()
            band_copies[chunk + 1].wait()
        hi, lo = split(band[at, :])
        col_t[at, :] = mm(hi, hot_rows) + mm(lo, hot_rows)
        term = mm(hot[:, at], hi) + mm(hot[:, at], lo)
        part = term if part is None else part + term
    row_t[...] = part.T
    last = col_t[pl.ds(3, TILES * LOCI, stride=Q), :]
    for a in range(3):
        diff = col_t[pl.ds(a, TILES * LOCI, stride=Q), :] - last
        place = slice(a * LOCI, (a + 1) * LOCI)
        for e in range(DEPTH):
            core_ref[e, place, :] = diff[(2 * e + 1) * LOCI : (2 * e + 2) * LOCI]
            value = diff[(2 * e + 2) * LOCI : (2 * e + 3) * LOCI]
            if e == DEPTH - 1:
                value = jnp.where(dead, 0.0, value)
            mine_ref[e, place, :] = value
    for step in range(COLS):
        start = (col_at ^ step) * PIECE
        to = keep_ref if step < NEAR else give_ref
        last = row_t[pl.ds(start + 3, LOCI, stride=Q), :]
        for a in range(3):
            place = slice(a * LOCI, (a + 1) * LOCI)
            to[step % NEAR, place, :] = row_t[pl.ds(start + a, LOCI, stride=Q), :] - last


def place_of():
    row_at = lax.axis_index("row")
    return row_at, lax.rem(row_at, 2) == 1, lax.rem(row_at // 2, DEPTH)


def combine_kernel(mine_ref, core_ref, keep_ref, got_ref, z_ref, last_ref, *part_refs):
    _, odd, z_at = place_of()
    for d in range(DEPTH + 1):
        lower = core_ref[d] if d < DEPTH else jnp.zeros((SENT, BATCH), f32)
        upper = core_ref[d - 1] if d else jnp.zeros((SENT, BATCH), f32)
        value = jnp.where(odd, lower, upper)
        if d:
            value = value + mine_ref[d - 1]
        if d < DEPTH:
            z_ref[lax.rem(z_at + d, DEPTH)] = value
        else:
            last_ref[...] = value
    for step in range(NEAR):
        part_refs[step][...] = keep_ref[step] + got_ref[step]


def sum_kernel(z_ref, last_ref, *rest):
    row_refs, out_ref = rest[:NEAR], rest[NEAR]
    _, _, z_at = place_of()
    own = row_refs[0][...]
    for step in range(1, NEAR):
        own = own + row_refs[step][...]
    other = last_ref[...]
    for s in range(DEPTH):
        part = z_ref[s]
        own = own + jnp.where(s <= z_at, part, 0.0)
        other = other + jnp.where(s > z_at, part, 0.0)
    out_ref[:SENT, :] = own
    out_ref[SENT:, :] = other


def choose_kernel(z_ref, other_ref, core_ref):
    _, odd, z_at = place_of()
    for e in range(DEPTH):
        lower = z_ref[lax.rem(z_at + e, DEPTH)]
        upper = z_ref[lax.rem(z_at + e + 1, DEPTH)] if e < DEPTH - 1 else other_ref[...]
        core_ref[e] = jnp.where(odd, lower, upper)


def flip_kernel(hot_ref, hot_rows_ref, hot_t_ref, hot_rows_t_ref):
    eye = (iota((128, 128), 0) == iota((128, 128), 1)).astype(f32).astype(bf16)
    for j in range(9):
        at = slice(j * 128, min(BAND, (j + 1) * 128))
        turned = lax.dot_general(
            hot_ref[:, at], eye, (((0,), (0,)), ((), ())), preferred_element_type=f32
        )
        hot_t_ref[at, :] = turned.astype(bf16)
    turned = lax.dot_general(eye, hot_rows_ref[...], NT, preferred_element_type=f32)
    hot_rows_t_ref[...] = turned.astype(bf16)


def pair_kernel(own_ref, got_ref, out_ref):
    out_ref[0] = own_ref[...]
    out_ref[1] = got_ref[...]


def softmax_kernel(
    here_ref, there_ref, codes_ref, fields_ref, z_ref, row_ref, other_ref, new_fields_ref
):
    row_at = lax.axis_index("row")
    col_at = lax.axis_index("col")
    z_at = lax.rem(row_at // 2, DEPTH)
    lane = iota((LOCI, 128), 1)
    locus = iota((LOCI, 128), 0)
    start = col_at % 2 * PIECE
    own = []
    other = []
    columns = []
    for block in range(2):
        block_at = lax.rem(row_at + block * HALF, ROWS)
        line = fields_ref[pl.ds(block_at * 4 + col_at // 2, 1), :]
        columns = [
            jnp.sum(jnp.where(lane == start + locus * Q + a, line, 0.0), axis=1, keepdims=True)
            for a in range(Q)
        ]
        if block == 0:
            own_columns = columns
        diffs = []
        for a in range(3):
            here = here_ref[block * SENT + a * LOCI : block * SENT + (a + 1) * LOCI, :]
            flip = (1 - block) * SENT + a * LOCI
            there = there_ref[flip : flip + LOCI, :]
            diffs.append(here + there + (columns[a] - columns[3]))
        highest = jnp.maximum(jnp.maximum(diffs[0], diffs[1]), jnp.maximum(diffs[2], 0.0))
        expon = [jnp.exp(d - highest) for d in diffs]
        total = expon[0] + expon[1] + expon[2] + jnp.exp(-highest)
        codes = codes_ref[block]
        resid = [
            jnp.where(codes == float(a), 1.0, 0.0) - expon[a] / total for a in range(3)
        ]
        if block == 0:
            own = resid
        else:
            other = resid
    sums = [jnp.sum(x, axis=1, keepdims=True) for x in own]
    sums.append(-(sums[0] + sums[1] + sums[2]))
    line = jnp.zeros((LOCI, 128), f32)
    for a in range(Q):
        value = own_columns[a] + step_rate * (sums[a] / BATCH - field_decay * own_columns[a])
        line = line + jnp.where(lane == locus * Q + a, value, 0.0)
    new_fields_ref[...] = jnp.sum(line, axis=0, keepdims=True)
    for a in range(3):
        place = slice(a * LOCI, (a + 1) * LOCI)
        other_ref[place, :] = other[a]
        row_ref[place, :] = own[a]
        for s in range(DEPTH):
            z_ref[s, place, :] = jnp.where(z_at >= s, own[a], other[a])


def update_kernel(band_ref, z_ref, other_ref, core_ref, hot_cols_ref, hot_rows_ref, *rest):
    row_refs, (out_ref, rows, cols, new_ref, sems) = rest[:NEAR], rest[NEAR:]
    row_at = lax.axis_index("row")
    col_at = lax.axis_index("col")
    z_at = lax.rem(row_at // 2, DEPTH)
    for j in range(TILES):
        if j % 2:
            part = core_ref[j // 2]
        elif j < HALF:
            part = z_ref[lax.rem(z_at + j // 2, DEPTH)]
        else:
            part = other_ref[...]
        pieces = [part[a * LOCI : (a + 1) * LOCI] for a in range(3)]
        pieces.append(-(pieces[0] + pieces[1] + pieces[2]))
        for a in range(Q):
            cols[pl.ds(j * PIECE + a, LOCI, stride=Q), :] = pieces[a]
    for step in range(COLS):
        part = row_refs[step % NEAR][step // NEAR]
        pieces = [part[a * LOCI : (a + 1) * LOCI, :] for a in range(3)]
        pieces.append(-(pieces[0] + pieces[1] + pieces[2]))
        for a in range(Q):
            at = (col_at ^ step) * PIECE + a
            rows[pl.ds(at, LOCI, stride=Q), :] = pieces[a]
    rows_hi, rows_lo = split(rows[...].T)
    right = jnp.concatenate([rows_hi, rows_lo, hot_rows_ref[...], hot_rows_ref[...]], axis=0)
    dead = row_at >= HALF
    copies = []
    for chunk, at in enumerate(CHUNKS):
        cols_hi, cols_lo = split(cols[at, :])
        hot = hot_cols_ref[at, :]
        gradient = mm(jnp.concatenate([hot, hot, cols_hi, cols_lo], axis=1), right)
        band = band_ref[at, :]
        spot = iota(band.shape, 0) + at.start
        if chunk == 0:
            same = (spot < PIECE) & ((col_at * PIECE + spot) // Q == iota(band.shape, 1) // Q)
            gradient = jnp.where(same, 0.0, gradient)
        new = band + step_rate * (gradient / BATCH - coupling_decay * band)
        if chunk == len(CHUNKS) - 1:
            new = jnp.where(dead & (spot >= HALF * PIECE), 0.0, new)
        new_ref[at, :] = new
        copies.append(pltpu.make_async_copy(new_ref.at[at], out_ref.at[at], sems.at[chunk]))
        copies[-1].start()
    for copy in copies:
        copy.wait()


def call(kernel, outs, scratch=(), name=None, hbm=False, hbm_out=False):
    specs = {"in_specs": [pl.BlockSpec(memory_space=pltpu.HBM)] * 2} if hbm else {}
    if hbm_out:
        specs["out_specs"] = pl.BlockSpec(memory_space=pltpu.HBM)
    return pl.pallas_call(
        kernel,
        out_shape=outs,
        scratch_shapes=list(scratch),
        compiler_params=pltpu.CompilerParams(
            vmem_limit_bytes=(52 if hbm else 24) * 1024 * 1024
        ),
        name=name,
        **specs,
    )


def arr(*shape, dtype=f32):
    return jax.ShapeDtypeStruct(shape, dtype)


def shards(seqs, fields, band):
    band_t = band.T
    piece = arr(SENT, BATCH)
    four = arr(NEAR, SENT, BATCH)
    eight = arr(DEPTH, SENT, BATCH)
    codes, mine, core, keep, give, hot, hot_rows = call(
        logits_kernel,
        (
            arr(2, LOCI, BATCH),
            eight,
            eight,
            four,
            four,
            arr(BATCH, 9 * 128, dtype=bf16),
            arr(SPAN, BATCH, dtype=bf16),
        ),
        [
            pltpu.VMEM((TILES, BATCH, 128), jnp.int32),
            pltpu.VMEM((BAND, SPAN), f32),
            pltpu.VMEM((SPAN, BATCH), f32),
            pltpu.VMEM((BAND, BATCH), f32),
            pltpu.SemaphoreType.DMA((TILES,)),
            pltpu.SemaphoreType.DMA((len(CHUNKS),)),
        ],
        "logit_parts",
        hbm=True,
    )(seqs, band_t)
    core = lax.ppermute(core, "row", SWAP_CORES)
    give = swap_cols(give, NEAR)
    z_send, last, *parts = call(
        combine_kernel, (eight, piece) + (piece,) * NEAR, name="combine"
    )(mine, core, keep, give)
    z_got = lax.all_to_all(z_send, "row", 0, 0, tiled=True, axis_index_groups=Z_GROUPS)
    row_got = [parts[0]] + [swap_cols(parts[step], step) for step in range(1, NEAR)]
    hot_cols, hot_rows = call(
        flip_kernel, (arr(BAND, BATCH, dtype=bf16), arr(BATCH, SPAN, dtype=bf16)), name="flip"
    )(hot, hot_rows)
    here = call(sum_kernel, arr(2 * SENT, BATCH), name="sum_parts")(z_got, last, *row_got)
    there = lax.ppermute(here, "row", SWAP_HALVES)
    z_send, resid, other, new_fields = call(
        softmax_kernel,
        (eight, piece, piece, arr(1, 128)),
        name="softmax",
    )(here, there, codes, fields.reshape(-1, 128))
    across = swap_cols(resid, NEAR)
    z_all = lax.all_to_all(z_send, "row", 0, 0, tiled=True, axis_index_groups=Z_GROUPS)
    pair = call(pair_kernel, arr(2, SENT, BATCH), name="pair")(resid, across)
    row_all = [pair] + [swap_cols(pair, step) for step in range(1, NEAR)]
    core_all = lax.ppermute(
        call(choose_kernel, eight, name="choose")(z_all, other), "row", SWAP_CORES
    )
    new_band_t = call(
        update_kernel,
        arr(BAND, SPAN),
        [
            pltpu.VMEM((SPAN, BATCH), f32),
            pltpu.VMEM((BAND, BATCH), f32),
            pltpu.VMEM((BAND, SPAN), f32),
            pltpu.SemaphoreType.DMA((len(CHUNKS),)),
        ],
        "update",
        hbm_out=True,
    )(band_t, z_all, other, core_all, hot_cols, hot_rows, *row_all)
    return new_band_t.T, new_fields[0, :PIECE]


def solution(mesh):
    in_specs = (P(), P(), P("row", "col"))
    out_specs = (P("row", "col"), P(("row", "col")))
    return jax.shard_map(shards, mesh=mesh, in_specs=in_specs, out_specs=out_specs, check_vma=False)
```

time: 78.1 us -> 57.1 us (0.73)
  blocking collectives: 44.7 us -> 0 us
  starting transfers between devices: 7.52 us -> 32.7 us
  local copies, waits for them, and re-layouts: 5.32 us -> 0.52 us
  Pallas kernels: 5.37 us -> 7.79 us
  waiting for transfers between devices: 14.1 us -> 15.1 us
    all_to_all x3 -> x0, blocking collectives: 44.7 us -> none  [the longest x1 24.8 us: shards(): lax.all_to_all(col_send, 'row', 0, 0, tiled=True, axis_index_groups=LOW_G...]
    ppermute x0 -> x10, starting transfers between devices: none -> 17.4 us  [the longest x8 8.41 us: swap_cols(): return lax.ppermute(x, 'col', [(i, i ^ step) for i in range(COLS)])]
    ppermute x0 -> x10, waiting for transfers between devices: none -> 10.2 us  [the longest x8 9.65 us: swap_cols(): return lax.ppermute(x, 'col', [(i, i ^ step) for i in range(COLS)])]
    all_to_all x1 -> x2, waiting for transfers between devices: 11.9 us -> 3.2 us  [shards(): lax.all_to_all(z_send, 'row', 0, 0, tiled=True, axis_index_groups=Z_GROUPS)]
    all_to_all x1 -> x2, starting transfers between devices: 4.98 us -> 12.4 us  [shards(): lax.all_to_all(z_send, 'row', 0, 0, tiled=True, axis_index_groups=Z_GROUPS)]
    unnamed x10 -> x4, local copies, waits for them, and re-layouts: 4.81 us -> 0.01 us
    pallas_call x3 -> x6, Pallas kernels: 2.98 us -> 5.87 us  [the longest x1 3.99 us: shards(): call(logits_kernel, (arr(2, LOCI, BATCH), eight, eight, four, four, arr(B...]
  transfers between devices with their start and end apart: 2 -> 13, of which waited for: 2 -> 8; matrix products, arithmetic and copies ran while one was open for 1% -> 1% of each run, Pallas kernels for 1% -> 1%
where the time goes in v2:
time: 57.1 us; the launch traced here: 56.8 us
  starting transfers between devices  32.7 us (57%)
  waiting for transfers between devices  15.1 us (26%)
  Pallas kernels  7.79 us (14%)
  between operations  0.69 us (1%)
    all_to_all x2, starting transfers between devices, shards(): lax.all_to_all(z_send, 'row', 0, 0, tiled=True, axis_index_groups=Z_GROUPS)  12.4 us
    ppermute x8, waiting for transfers between devices, swap_cols(): return lax.ppermute(x, 'col', [(i, i ^ step) for i in range(COLS)])  9.65 us
    ppermute x8, starting transfers between devices, swap_cols(): return lax.ppermute(x, 'col', [(i, i ^ step) for i in range(COLS)])  8.41 us
    ppermute x1, starting transfers between devices, shards(): lax.ppermute(call(choose_kernel, eight, name='choose')(z_all, other), 'ro...  5.68 us
    pallas_call x1, Pallas kernels, shards(): call(logits_kernel, (arr(2, LOCI, BATCH), eight, eight, four, four, arr(B...  3.99 us
    ppermute x1, starting transfers between devices, shards(): core = lax.ppermute(core, 'row', SWAP_CORES)  3.33 us
    all_to_all x2, waiting for transfers between devices, shards(): lax.all_to_all(z_send, 'row', 0, 0, tiled=True, axis_index_groups=Z_GROUPS)  3.2 us
    ppermute x1, starting transfers between devices, shards(): there = lax.ppermute(here, 'row', SWAP_HALVES)  2.84 us
  transfers between devices with their start and end apart: 13, of which 8 were waited for; matrix products, arithmetic and copies ran while one was open for 1% of the time, Pallas kernels for 1%

profile of v2, /device:TPU:1, one launch (start us, length us, event | category | flops | bytes accessed | tf_op | source)
XLA Modules:
  0.0 56.8 jit_solution(4483247972467058197)
XLA Ops:
  0.6 4.0 %logit_parts.1 = (f32[2,16,128]{2,1,0:T(8,128)S(1)}, f32[8,48,128]{2,1,0:T(8,128)S(1)}, f32[8,48,128]{2,1,0:T(8,128)S(1)}, f32[4,48,128]{2,1,0:T(8,128)S(1)}, f3...) custom-call(s32[128,4096]{1,0:T(8,128)} %seqs_ref.1, f32[1088,512]{1,0:T(8,128)} %bitcast.5), custom_call_target="tpu_custom_call" | custom-call | tf_op jit(solution)/shard_map/logit_parts/pallas_call | solution.py:331
  4.6 0.0 copy-start
  4.6 3.3 %collective-permute-start = (f32[8,48,128]{2,1,0:T(8,128)S(1)}, f32[8,48,128]{2,1,0:T(8,128)S(1)}, u32[]{:S(2)}, u32[]{:S(2)}) collective-permute-start(f32[8,48,128]{2,1,0:T(8,128)S(1)} %get-tuple-element.22), channel_id=1, source_target_pairs={{0,8},{8,0},{16,24},{24,16},{32,40},{40,32},{48,56},{56,48},{64,72... | collective-permute-start | bytes 589832 | tf_op jit(solution)/shard_map/ppermute | solution.py:353
  8.0 0.0 collective-permute-start.1
  8.0 4.4 %collective-permute-done.1.got_ref = f32[4,48,128]{2,1,0:T(8,128)S(1)} collective-permute-done((f32[4,48,128]{2,1,0:T(8,128)S(1)}, f32[4,48,128]{2,1,0:T(8,128)S(1)}, u32[]{:S(2)}, u32[]{:S(2)}) %collective-permute-start.1) | collective-permute-done | bytes 98336 | tf_op jit(solution)/shard_map/ppermute | solution.py:31
  12.3 0.0 collective-permute-done.core_ref
  12.3 0.7 %combine.1 = (f32[8,48,128]{2,1,0:T(8,128)}, f32[48,128]{1,0:T(8,128)S(1)}, f32[48,128]{1,0:T(8,128)S(1)}, f32[48,128]{1,0:T(8,128)S(1)}, f32[48,128]{1,0:T(8,128)S(1)}, /*index=5*/f32[48,128]{1,0:T(8,128)S(1)}) custom-call(f32[8,48,128]{2,1,0:T(8,128)S(1)} %get-tuple-element.21.mine_ref, f32[8,48,128]{2,1,0:T(8,128)S(1)} %collective-permute-done.core_ref, ...), custom_call_target="tpu_custom_call" | custom-call | tf_op jit(solution)/shard_map/combine/pallas_call | solution.py:355
  13.1 6.4 %all-to-all-start = ((f32[8,48,128]{2,1,0:T(8,128)}), f32[8,48,128]{2,1,0:T(8,128)S(1)}, u32[]{:S(2)}, u32[]{:S(2)}) async-start(f32[8,48,128]{2,1,0:T(8,128)} %get-tuple-element.25), calls=%async_computation | async-start | bytes 393216 | tf_op jit(solution)/shard_map/all_to_all | solution.py:358
  19.5 1.3 %collective-permute-start.2 = (f32[48,128]{1,0:T(8,128)S(1)}, f32[48,128]{1,0:T(8,128)S(1)}, u32[]{:S(2)}, u32[]{:S(2)}) collective-permute-start(f32[48,128]{1,0:T(8,128)S(1)} %get-tuple-element.28), channel_id=1, source_target_pairs={{0,1},{1,0},{2,3},{3,2},{4,5},{5,4},{6,7},{7,6},{8,9},{9,8},{10,11... | collective-permute-start | bytes 73736 | tf_op jit(solution)/shard_map/ppermute | solution.py:31
  20.8 2.6 %collective-permute-start.3 = (f32[48,128]{1,0:T(8,128)S(1)}, f32[48,128]{1,0:T(8,128)S(1)}, u32[]{:S(2)}, u32[]{:S(2)}) collective-permute-start(f32[48,128]{1,0:T(8,128)S(1)} %get-tuple-element.29), channel_id=1, source_target_pairs={{0,2},{1,3},{2,0},{3,1},{4,6},{5,7},{6,4},{7,5},{8,10},{9,11},{10,... | collective-permute-start | bytes 73736 | tf_op jit(solution)/shard_map/ppermute | solution.py:31
  23.4 0.0 collective-permute-start.4
  23.4 0.0 collective-permute-done.2.rest_1_
  23.4 1.5 %collective-permute-done.3.rest_2_ = f32[48,128]{1,0:T(8,128)S(1)} collective-permute-done((f32[48,128]{1,0:T(8,128)S(1)}, f32[48,128]{1,0:T(8,128)S(1)}, u32[]{:S(2)}, u32[]{:S(2)}) %collective-permute-start.3) | collective-permute-done | bytes 24608 | tf_op jit(solution)/shard_map/ppermute | solution.py:31
  25.0 2.6 %collective-permute-done.4.rest_3_ = f32[48,128]{1,0:T(8,128)S(1)} collective-permute-done((f32[48,128]{1,0:T(8,128)S(1)}, f32[48,128]{1,0:T(8,128)S(1)}, u32[]{:S(2)}, u32[]{:S(2)}) %collective-permute-start.4) | collective-permute-done | bytes 24608 | tf_op jit(solution)/shard_map/ppermute | solution.py:31
  27.6 0.5 all-to-all-done.z_ref
  28.1 0.1 sum_parts.1.here_ref
  28.2 2.8 %collective-permute-start.5 = (f32[96,128]{1,0:T(8,128)S(1)}, f32[96,128]{1,0:T(8,128)S(1)}, u32[]{:S(2)}, u32[]{:S(2)}) collective-permute-start(f32[96,128]{1,0:T(8,128)S(1)} %sum_parts.1.here_ref), channel_id=1, source_target_pairs={{0,128},{8,136},{16,144},{24,152},{32,160},{40,168},{48,176},{56,1... | collective-permute-start | bytes 147464 | tf_op jit(solution)/shard_map/ppermute | solution.py:364
  31.0 1.7 %collective-permute-done.5.there_ref = f32[96,128]{1,0:T(8,128)S(1)} collective-permute-done((f32[96,128]{1,0:T(8,128)S(1)}, f32[96,128]{1,0:T(8,128)S(1)}, u32[]{:S(2)}, u32[]{:S(2)}) %collective-permute-start.5) | collective-permute-done | bytes 49184 | tf_op jit(solution)/shard_map/ppermute | solution.py:364
  32.7 0.8 %softmax.1 = (f32[8,48,128]{2,1,0:T(8,128)}, f32[48,128]{1,0:T(8,128)S(1)}, f32[48,128]{1,0:T(8,128)S(1)}, f32[1,128]{1,0:T(1,128)S(1)}) custom-call(f32[96,128]{1,0:T(8,128)S(1)} %sum_parts.1.here_ref, f32[96,128]{1,0:T(8,128)S(1)} %collective-permute-done.5.there_ref, f32[2,16,128]{2,1,0:T(8,128)S(1)} %get-tuple-element.31.codes_ref, f32[128,128]{1,0:T(8,128)S(1)} %bitcast.7), custom_call_target="tpu_custom_call" | custom-call | tf_op jit(solution)/shard_map/softmax/pallas_call | solution.py:365
  33.5 6.0 %all-to-all-start.1 = ((f32[8,48,128]{2,1,0:T(8,128)}), f32[8,48,128]{2,1,0:T(8,128)S(1)}, u32[]{:S(2)}, u32[]{:S(2)}) async-start(f32[8,48,128]{2,1,0:T(8,128)} %get-tuple-element.32), calls=%async_computation.1 | async-start | bytes 393216 | tf_op jit(solution)/shard_map/all_to_all | solution.py:371
  39.5 1.2 %collective-permute-start.7 = (f32[48,128]{1,0:T(8,128)S(1)}, f32[48,128]{1,0:T(8,128)S(1)}, u32[]{:S(2)}, u32[]{:S(2)}) collective-permute-start(f32[48,128]{1,0:T(8,128)S(1)} %get-tuple-element.38.own_ref), channel_id=1, source_target_pairs={{0,4},{1,5},{2,6},{3,7},{4,0},{5,1},{6,2},{7,3},{8,12},{9,13},{10,... | collective-permute-start | bytes 73736 | tf_op jit(solution)/shard_map/ppermute | solution.py:31
  40.7 0.3 flip.1
  41.1 1.1 %collective-permute-done.7.got_ref = f32[48,128]{1,0:T(8,128)S(1)} collective-permute-done((f32[48,128]{1,0:T(8,128)S(1)}, f32[48,128]{1,0:T(8,128)S(1)}, u32[]{:S(2)}, u32[]{:S(2)}) %collective-permute-start.7) | collective-permute-done | bytes 24608 | tf_op jit(solution)/shard_map/ppermute | solution.py:31
  42.2 0.3 collective-permute-start.10
  42.4 0.4 collective-permute-start.9
  42.8 2.6 %collective-permute-start.8 = (f32[2,48,128]{2,1,0:T(8,128)S(1)}, f32[2,48,128]{2,1,0:T(8,128)S(1)}, u32[]{:S(2)}, u32[]{:S(2)}) collective-permute-start(f32[2,48,128]{2,1,0:T(8,128)S(1)} %pair.1.rest_0_), channel_id=1, source_target_pairs={{0,1},{1,0},{2,3},{3,2},{4,5},{5,4},{6,7},{7,6},{8,9},{9,8},{10,11... | collective-permute-start | bytes 147464 | tf_op jit(solution)/shard_map/ppermute | solution.py:31
  45.4 2.7 %all-to-all-done.1.z_ref = f32[8,48,128]{2,1,0:T(8,128)S(1)} async-done(((f32[8,48,128]{2,1,0:T(8,128)}), f32[8,48,128]{2,1,0:T(8,128)S(1)}, u32[]{:S(2)}, u32[]{:S(2)}) %all-to-all-start.1) | async-done | bytes 196640 | tf_op jit(solution)/shard_map/all_to_all | solution.py:371
  48.2 5.7 %collective-permute-start.6 = (f32[8,48,128]{2,1,0:T(8,128)S(1)}, f32[8,48,128]{2,1,0:T(8,128)S(1)}, u32[]{:S(2)}, u32[]{:S(2)}) collective-permute-start(f32[8,48,128]{2,1,0:T(8,128)S(1)} %choose.1), channel_id=1, source_target_pairs={{0,8},{8,0},{16,24},{24,16},{32,40},{40,32},{48,56},{56,48},{64,72... | collective-permute-start | bytes 589832 | tf_op jit(solution)/shard_map/ppermute | solution.py:374
  53.8 0.5 slice_bitcast_fusion
  54.3 0.0 collective-permute-done.10.rest_3_
  54.4 0.5 collective-permute-done.6.core_ref
  54.9 1.9 %update.1 = f32[1088,512]{1,0:T(8,128)} custom-call(f32[1088,512]{1,0:T(8,128)S(1)} %bitcast.6, f32[8,48,128]{2,1,0:T(8,128)S(1)} %all-to-all-done.1.z_ref, f32[48,128]{1,0:T(8,128)S(1)} %get-tuple-element.33.other_ref, f32[8,48,128]{2,1,0:T(8,128)S(1)} %collective-permute-done.6.core_ref, bf16[1088,128]{1,0:T(8,128)(2,1)S(1)} %get-tuple-element.36.hot_cols_ref, ...), custom_call_target="tpu_custom_call" | custom-call | tf_op jit(solution)/shard_map/update/pallas_call | solution.py:377
  (7 shorter events, 0.0 us)
Async XLA Ops:
  0.6 32.1 %copy-start.1 = (f32[16384]{0:T(1024)S(1)}, f32[16384]{0:T(1024)}, u32[]{:S(2)}) copy-start(f32[16384]{0:T(1024)} %param.4) | copy-start | bytes 196612
  4.6 50.3 %copy-start = (f32[512,1088]{0,1:T(8,128)S(1)}, f32[512,1088]{0,1:T(8,128)}, u32[]{:S(2)}) copy-start(f32[512,1088]{0,1:T(8,128)} %param.5) | copy-start | bytes 6684676
  4.6 7.7 %collective-permute-start = (f32[8,48,128]{2,1,0:T(8,128)S(1)}, f32[8,48,128]{2,1,0:T(8,128)S(1)}, u32[]{:S(2)}, u32[]{:S(2)}) collective-permute-start(f32[8,48,128]{2,1,0:T(8,128)S(1)} %get-tuple-element.22), channel_id=1, source_target_pairs={{0,8},{8,0},{16,24},{24,16},{32,40},{40,32},{48,56},{56,48},{64,72... | collective-permute-start | bytes 589832 | tf_op jit(solution)/shard_map/ppermute | solution.py:353
  8.0 4.4 %collective-permute-start.1 = (f32[4,48,128]{2,1,0:T(8,128)S(1)}, f32[4,48,128]{2,1,0:T(8,128)S(1)}, u32[]{:S(2)}, u32[]{:S(2)}) collective-permute-start(f32[4,48,128]{2,1,0:T(8,128)S(1)} %get-tuple-element.24), channel_id=1, source_target_pairs={{0,4},{1,5},{2,6},{3,7},{4,0},{5,1},{6,2},{7,3},{8,12},{9,13},{10,... | collective-permute-start | bytes 294920 | tf_op jit(solution)/shard_map/ppermute | solution.py:31
  13.1 15.1 %all-to-all-start = ((f32[8,48,128]{2,1,0:T(8,128)}), f32[8,48,128]{2,1,0:T(8,128)S(1)}, u32[]{:S(2)}, u32[]{:S(2)}) async-start(f32[8,48,128]{2,1,0:T(8,128)} %get-tuple-element.25), calls=%async_computation | async-start | bytes 393216 | tf_op jit(solution)/shard_map/all_to_all | solution.py:358
  19.5 3.9 %collective-permute-start.2 = (f32[48,128]{1,0:T(8,128)S(1)}, f32[48,128]{1,0:T(8,128)S(1)}, u32[]{:S(2)}, u32[]{:S(2)}) collective-permute-start(f32[48,128]{1,0:T(8,128)S(1)} %get-tuple-element.28), channel_id=1, source_target_pairs={{0,1},{1,0},{2,3},{3,2},{4,5},{5,4},{6,7},{7,6},{8,9},{9,8},{10,11... | collective-permute-start | bytes 73736 | tf_op jit(solution)/shard_map/ppermute | solution.py:31
  20.8 4.2 %collective-permute-start.3 = (f32[48,128]{1,0:T(8,128)S(1)}, f32[48,128]{1,0:T(8,128)S(1)}, u32[]{:S(2)}, u32[]{:S(2)}) collective-permute-start(f32[48,128]{1,0:T(8,128)S(1)} %get-tuple-element.29), channel_id=1, source_target_pairs={{0,2},{1,3},{2,0},{3,1},{4,6},{5,7},{6,4},{7,5},{8,10},{9,11},{10,... | collective-permute-start | bytes 73736 | tf_op jit(solution)/shard_map/ppermute | solution.py:31
  23.4 4.2 %collective-permute-start.4 = (f32[48,128]{1,0:T(8,128)S(1)}, f32[48,128]{1,0:T(8,128)S(1)}, u32[]{:S(2)}, u32[]{:S(2)}) collective-permute-start(f32[48,128]{1,0:T(8,128)S(1)} %get-tuple-element.30), channel_id=1, source_target_pairs={{0,3},{1,2},{2,1},{3,0},{4,7},{5,6},{6,5},{7,4},{8,11},{9,10},{10,... | collective-permute-start | bytes 73736 | tf_op jit(solution)/shard_map/ppermute | solution.py:31
  28.2 4.5 %collective-permute-start.5 = (f32[96,128]{1,0:T(8,128)S(1)}, f32[96,128]{1,0:T(8,128)S(1)}, u32[]{:S(2)}, u32[]{:S(2)}) collective-permute-start(f32[96,128]{1,0:T(8,128)S(1)} %sum_parts.1.here_ref), channel_id=1, source_target_pairs={{0,128},{8,136},{16,144},{24,152},{32,160},{40,168},{48,176},{56,1... | collective-permute-start | bytes 147464 | tf_op jit(solution)/shard_map/ppermute | solution.py:364
  33.5 14.6 %all-to-all-start.1 = ((f32[8,48,128]{2,1,0:T(8,128)}), f32[8,48,128]{2,1,0:T(8,128)S(1)}, u32[]{:S(2)}, u32[]{:S(2)}) async-start(f32[8,48,128]{2,1,0:T(8,128)} %get-tuple-element.32), calls=%async_computation.1 | async-start | bytes 393216 | tf_op jit(solution)/shard_map/all_to_all | solution.py:371
  39.5 2.7 %collective-permute-start.7 = (f32[48,128]{1,0:T(8,128)S(1)}, f32[48,128]{1,0:T(8,128)S(1)}, u32[]{:S(2)}, u32[]{:S(2)}) collective-permute-start(f32[48,128]{1,0:T(8,128)S(1)} %get-tuple-element.38.own_ref), channel_id=1, source_target_pairs={{0,4},{1,5},{2,6},{3,7},{4,0},{5,1},{6,2},{7,3},{8,12},{9,13},{10,... | collective-permute-start | bytes 73736 | tf_op jit(solution)/shard_map/ppermute | solution.py:31
  42.2 12.2 %collective-permute-start.10 = (f32[2,48,128]{2,1,0:T(8,128)S(1)}, f32[2,48,128]{2,1,0:T(8,128)S(1)}, u32[]{:S(2)}, u32[]{:S(2)}) collective-permute-start(f32[2,48,128]{2,1,0:T(8,128)S(1)} %pair.1.rest_0_), channel_id=1, source_target_pairs={{0,3},{1,2},{2,1},{3,0},{4,7},{5,6},{6,5},{7,4},{8,11},{9,10},{10,... | collective-permute-start | bytes 147464 | tf_op jit(solution)/shard_map/ppermute | solution.py:31
  42.4 11.9 %collective-permute-start.9 = (f32[2,48,128]{2,1,0:T(8,128)S(1)}, f32[2,48,128]{2,1,0:T(8,128)S(1)}, u32[]{:S(2)}, u32[]{:S(2)}) collective-permute-start(f32[2,48,128]{2,1,0:T(8,128)S(1)} %pair.1.rest_0_), channel_id=1, source_target_pairs={{0,2},{1,3},{2,0},{3,1},{4,6},{5,7},{6,4},{7,5},{8,10},{9,11},{10,... | collective-permute-start | bytes 147464 | tf_op jit(solution)/shard_map/ppermute | solution.py:31
  42.8 11.5 %collective-permute-start.8 = (f32[2,48,128]{2,1,0:T(8,128)S(1)}, f32[2,48,128]{2,1,0:T(8,128)S(1)}, u32[]{:S(2)}, u32[]{:S(2)}) collective-permute-start(f32[2,48,128]{2,1,0:T(8,128)S(1)} %pair.1.rest_0_), channel_id=1, source_target_pairs={{0,1},{1,0},{2,3},{3,2},{4,5},{5,4},{6,7},{7,6},{8,9},{9,8},{10,11... | collective-permute-start | bytes 147464 | tf_op jit(solution)/shard_map/ppermute | solution.py:31
  48.2 6.7 %collective-permute-start.6 = (f32[8,48,128]{2,1,0:T(8,128)S(1)}, f32[8,48,128]{2,1,0:T(8,128)S(1)}, u32[]{:S(2)}, u32[]{:S(2)}) collective-permute-start(f32[8,48,128]{2,1,0:T(8,128)S(1)} %choose.1), channel_id=1, source_target_pairs={{0,8},{8,0},{16,24},{24,16},{32,40},{40,32},{48,56},{56,48},{64,72... | collective-permute-start | bytes 589832 | tf_op jit(solution)/shard_map/ppermute | solution.py:374

commit v3 on v2

--- a/solution.py
+++ b/solution.py
@@ -22,7 +22,8 @@
 field_decay = 0.1
 
 DEPTH = 8
-Z_GROUPS = [[(h * DEPTH + z) * 2 + k for z in range(DEPTH)] for h in range(2) for k in range(2)]
+PLANES = [7, 6, 5, 4, 0, 1, 2, 3]
+Z_GROUPS = [[(h * DEPTH + z) * 2 + k for z in PLANES] for h in range(2) for k in range(2)]
 SWAP_CORES = [(i, i ^ 1) for i in range(ROWS)]
 SWAP_HALVES = [(i, i ^ HALF) for i in range(ROWS)]
 
@@ -143,6 +144,11 @@
             to[step % NEAR, place, :] = row_t[pl.ds(start + a, LOCI, stride=Q), :] - last
 
 
+def slot_of(z):
+    z = lax.rem(z, DEPTH)
+    return jnp.where(z < 4, z + 4, 7 - z)
+
+
 def place_of():
     row_at = lax.axis_index("row")
     return row_at, lax.rem(row_at, 2) == 1, lax.rem(row_at // 2, DEPTH)
@@ -157,14 +163,15 @@
         if d:
             value = value + mine_ref[d - 1]
         if d < DEPTH:
-            z_ref[lax.rem(z_at + d, DEPTH)] = value
+            z_ref[slot_of(z_at + d)] = value
         else:
             last_ref[...] = value
     for step in range(NEAR):
         part_refs[step][...] = keep_ref[step] + got_ref[step]
 
 
-def sum_kernel(z_ref, last_ref, *rest):
+def sum_kernel(z_ref, last_ref, hot_ref, hot_rows_ref, *rest):
+    del hot_ref, hot_rows_ref
     row_refs, out_ref = rest[:NEAR], rest[NEAR]
     _, _, z_at = place_of()
     own = row_refs[0][...]
@@ -172,7 +179,7 @@
         own = own + row_refs[step][...]
     other = last_ref[...]
     for s in range(DEPTH):
-        part = z_ref[s]
+        part = z_ref[PLANES.index(s)]
         own = own + jnp.where(s <= z_at, part, 0.0)
         other = other + jnp.where(s > z_at, part, 0.0)
     out_ref[:SENT, :] = own
@@ -182,8 +189,8 @@
 def choose_kernel(z_ref, other_ref, core_ref):
     _, odd, z_at = place_of()
     for e in range(DEPTH):
-        lower = z_ref[lax.rem(z_at + e, DEPTH)]
-        upper = z_ref[lax.rem(z_at + e + 1, DEPTH)] if e < DEPTH - 1 else other_ref[...]
+        lower = z_ref[slot_of(z_at + e)]
+        upper = z_ref[slot_of(z_at + e + 1)] if e < DEPTH - 1 else other_ref[...]
         core_ref[e] = jnp.where(odd, lower, upper)
 
 
@@ -254,47 +261,59 @@
         other_ref[place, :] = other[a]
         row_ref[place, :] = own[a]
         for s in range(DEPTH):
-            z_ref[s, place, :] = jnp.where(z_at >= s, own[a], other[a])
-
-
-def update_kernel(band_ref, z_ref, other_ref, core_ref, hot_cols_ref, hot_rows_ref, *rest):
-    row_refs, (out_ref, rows, cols, new_ref, sems) = rest[:NEAR], rest[NEAR:]
+            z_ref[PLANES.index(s), place, :] = jnp.where(z_at >= s, own[a], other[a])
+
+
+def fill(part, to_ref, at):
+    pieces = [part[a * LOCI : (a + 1) * LOCI] for a in range(3)]
+    pieces.append(-(pieces[0] + pieces[1] + pieces[2]))
+    for a in range(Q):
+        to_ref[pl.ds(at + a, LOCI, stride=Q), :] = pieces[a]
+
+
+def masked(gradient, at):
+    if at.start:
+        return gradient
+    col_at = lax.axis_index("col")
+    spot = iota(gradient.shape, 0)
+    same = (spot < PIECE) & ((col_at * PIECE + spot) // Q == iota(gradient.shape, 1) // Q)
+    return jnp.where(same, 0.0, gradient)
+
+
+def rows_kernel(band_ref, hot_cols_ref, *rest):
+    row_refs, (out_ref, rows) = rest[:NEAR], rest[NEAR:]
+    col_at = lax.axis_index("col")
+    for step in range(COLS):
+        fill(row_refs[step % NEAR][step // NEAR], rows, (col_at ^ step) * PIECE)
+    rows_hi, rows_lo = split(rows[...].T)
+    right = jnp.concatenate([rows_hi, rows_lo], axis=0)
+    for at in CHUNKS:
+        hot = hot_cols_ref[at, :]
+        gradient = masked(mm(jnp.concatenate([hot, hot], axis=1), right), at)
+        band = band_ref[at, :]
+        out_ref[at, :] = band + step_rate * (gradient / BATCH - coupling_decay * band)
+
+
+def cols_kernel(part_ref, z_ref, other_ref, core_ref, hot_rows_ref, out_ref, cols, new_ref, sems):
     row_at = lax.axis_index("row")
-    col_at = lax.axis_index("col")
     z_at = lax.rem(row_at // 2, DEPTH)
     for j in range(TILES):
         if j % 2:
             part = core_ref[j // 2]
         elif j < HALF:
-            part = z_ref[lax.rem(z_at + j // 2, DEPTH)]
+            part = z_ref[slot_of(z_at + j // 2)]
         else:
             part = other_ref[...]
-        pieces = [part[a * LOCI : (a + 1) * LOCI] for a in range(3)]
-        pieces.append(-(pieces[0] + pieces[1] + pieces[2]))
-        for a in range(Q):
-            cols[pl.ds(j * PIECE + a, LOCI, stride=Q), :] = pieces[a]
-    for step in range(COLS):
-        part = row_refs[step % NEAR][step // NEAR]
-        pieces = [part[a * LOCI : (a + 1) * LOCI, :] for a in range(3)]
-        pieces.append(-(pieces[0] + pieces[1] + pieces[2]))
-        for a in range(Q):
-            at = (col_at ^ step) * PIECE + a
-            rows[pl.ds(at, LOCI, stride=Q), :] = pieces[a]
-    rows_hi, rows_lo = split(rows[...].T)
-    right = jnp.concatenate([rows_hi, rows_lo, hot_rows_ref[...], hot_rows_ref[...]], axis=0)
+        fill(part, cols, j * PIECE)
+    hot_rows = hot_rows_ref[...]
+    right = jnp.concatenate([hot_rows, hot_rows], axis=0)
     dead = row_at >= HALF
     copies = []
     for chunk, at in enumerate(CHUNKS):
-        cols_hi, cols_lo = split(cols[at, :])
-        hot = hot_cols_ref[at, :]
-        gradient = mm(jnp.concatenate([hot, hot, cols_hi, cols_lo], axis=1), right)
-        band = band_ref[at, :]
-        spot = iota(band.shape, 0) + at.start
-        if chunk == 0:
-            same = (spot < PIECE) & ((col_at * PIECE + spot) // Q == iota(band.shape, 1) // Q)
-            gradient = jnp.where(same, 0.0, gradient)
-        new = band + step_rate * (gradient / BATCH - coupling_decay * band)
+        gradient = masked(mm(jnp.concatenate(split(cols[at, :]), axis=1), right), at)
+        new = part_ref[at, :] + step_rate * (gradient / BATCH)
         if chunk == len(CHUNKS) - 1:
+            spot = iota(new.shape, 0) + at.start
             new = jnp.where(dead & (spot >= HALF * PIECE), 0.0, new)
         new_ref[at, :] = new
         copies.append(pltpu.make_async_copy(new_ref.at[at], out_ref.at[at], sems.at[chunk]))
@@ -303,8 +322,15 @@
         copy.wait()
 
 
-def call(kernel, outs, scratch=(), name=None, hbm=False, hbm_out=False):
+COST = pl.CostEstimate(flops=4 * 10**10, bytes_accessed=10**6, transcendentals=0)
+
+
+def call(kernel, outs, scratch=(), name=None, hbm=False, hbm_out=False, cost=None, loose=(), inputs=0):
     specs = {"in_specs": [pl.BlockSpec(memory_space=pltpu.HBM)] * 2} if hbm else {}
+    if loose:
+        specs["in_specs"] = [
+            pl.BlockSpec(memory_space=pl.ANY if i in loose else pltpu.VMEM) for i in range(inputs)
+        ]
     if hbm_out:
         specs["out_specs"] = pl.BlockSpec(memory_space=pltpu.HBM)
     return pl.pallas_call(
@@ -315,6 +341,7 @@
             vmem_limit_bytes=(52 if hbm else 24) * 1024 * 1024
         ),
         name=name,
+        cost_estimate=cost,
         **specs,
     )
 
@@ -356,11 +383,13 @@
         combine_kernel, (eight, piece) + (piece,) * NEAR, name="combine"
     )(mine, core, keep, give)
     z_got = lax.all_to_all(z_send, "row", 0, 0, tiled=True, axis_index_groups=Z_GROUPS)
-    row_got = [parts[0]] + [swap_cols(parts[step], step) for step in range(1, NEAR)]
+    row_got = [swap_cols(parts[step], step) for step in (3, 2, 1)] + [parts[0]]
     hot_cols, hot_rows = call(
         flip_kernel, (arr(BAND, BATCH, dtype=bf16), arr(BATCH, SPAN, dtype=bf16)), name="flip"
     )(hot, hot_rows)
-    here = call(sum_kernel, arr(2 * SENT, BATCH), name="sum_parts")(z_got, last, *row_got)
+    here = call(sum_kernel, arr(2 * SENT, BATCH), name="sum_parts", loose=(2, 3), inputs=8)(
+        z_got, last, hot_cols, hot_rows, *row_got
+    )
     there = lax.ppermute(here, "row", SWAP_HALVES)
     z_send, resid, other, new_fields = call(
         softmax_kernel,
@@ -369,23 +398,25 @@
     )(here, there, codes, fields.reshape(-1, 128))
     across = swap_cols(resid, NEAR)
     z_all = lax.all_to_all(z_send, "row", 0, 0, tiled=True, axis_index_groups=Z_GROUPS)
-    pair = call(pair_kernel, arr(2, SENT, BATCH), name="pair")(resid, across)
+    pair = call(pair_kernel, arr(2, SENT, BATCH), name="pair", cost=COST)(resid, across)
     row_all = [pair] + [swap_cols(pair, step) for step in range(1, NEAR)]
     core_all = lax.ppermute(
         call(choose_kernel, eight, name="choose")(z_all, other), "row", SWAP_CORES
     )
+    part = call(
+        rows_kernel, arr(BAND, SPAN), [pltpu.VMEM((SPAN, BATCH), f32)], "update_rows"
+    )(band_t, hot_cols, *row_all)
     new_band_t = call(
-        update_kernel,
+        cols_kernel,
         arr(BAND, SPAN),
         [
-            pltpu.VMEM((SPAN, BATCH), f32),
             pltpu.VMEM((BAND, BATCH), f32),
             pltpu.VMEM((BAND, SPAN), f32),
             pltpu.SemaphoreType.DMA((len(CHUNKS),)),
         ],
-        "update",
+        "update_cols",
         hbm_out=True,
-    )(band_t, z_all, other, core_all, hot_cols, hot_rows, *row_all)
+    )(part, z_all, other, core_all, hot_rows)
     return new_band_t.T, new_fields[0, :PIECE]
 
 

time: 57.1 us -> 55.1 us (0.965)
  waiting for transfers between devices: 15.1 us -> 12.1 us
  starting transfers between devices: 32.7 us -> 33.3 us
    ppermute x8, waiting for transfers between devices: 9.65 us -> 7.88 us  [swap_cols(): return lax.ppermute(x, 'col', [(i, i ^ step) for i in range(COLS)])]
    all_to_all x2, starting transfers between devices: 12.4 us -> 13.5 us  [shards(): lax.all_to_all(z_send, 'row', 0, 0, tiled=True, axis_index_groups=Z_GROUPS)]
    all_to_all x2, waiting for transfers between devices: 3.2 us -> 2.5 us  [shards(): lax.all_to_all(z_send, 'row', 0, 0, tiled=True, axis_index_groups=Z_GROUPS)]
    pallas_call x3 -> x4, Pallas kernels: 1.92 us -> 2.34 us  [the longest x1 1.66 us: shards(): call(cols_kernel, arr(BAND, SPAN), [pltpu.VMEM((BAND, BATCH), f32), pltpu...]
  transfers between devices with their start and end apart: 13 -> 13, of which waited for: 8 -> 5; matrix products, arithmetic and copies ran while one was open for 1% -> 1% of each run, Pallas kernels for 1% -> 2%
where the time goes in v3:
time: 55.1 us; the launch traced here: 54.8 us
  starting transfers between devices  33.3 us (60%)
  waiting for transfers between devices  12.1 us (22%)
  Pallas kernels  8.21 us (15%)
  between operations  0.72 us (1%)
    all_to_all x2, starting transfers between devices, shards(): lax.all_to_all(z_send, 'row', 0, 0, tiled=True, axis_index_groups=Z_GROUPS)  13.5 us
    ppermute x8, starting transfers between devices, swap_cols(): return lax.ppermute(x, 'col', [(i, i ^ step) for i in range(COLS)])  7.89 us
    ppermute x8, waiting for transfers between devices, swap_cols(): return lax.ppermute(x, 'col', [(i, i ^ step) for i in range(COLS)])  7.88 us
    ppermute x1, starting transfers between devices, shards(): lax.ppermute(call(choose_kernel, eight, name='choose')(z_all, other), 'ro...  5.64 us
    pallas_call x1, Pallas kernels, shards(): call(logits_kernel, (arr(2, LOCI, BATCH), eight, eight, four, four, arr(B...  3.99 us
    ppermute x1, starting transfers between devices, shards(): core = lax.ppermute(core, 'row', SWAP_CORES)  3.33 us
    ppermute x1, starting transfers between devices, shards(): there = lax.ppermute(here, 'row', SWAP_HALVES)  2.84 us
    all_to_all x2, waiting for transfers between devices, shards(): lax.all_to_all(z_send, 'row', 0, 0, tiled=True, axis_index_groups=Z_GROUPS)  2.5 us
  transfers between devices with their start and end apart: 13, of which 5 were waited for; matrix products, arithmetic and copies ran while one was open for 1% of the time, Pallas kernels for 2%

profile of v3, /device:TPU:1, one launch (start us, length us, event | category | flops | bytes accessed | tf_op | source)
XLA Modules:
  0.0 54.8 jit_solution(7437569761860375254)
XLA Ops:
  0.6 4.0 %logit_parts.1 = (f32[2,16,128]{2,1,0:T(8,128)S(1)}, f32[8,48,128]{2,1,0:T(8,128)S(1)}, f32[8,48,128]{2,1,0:T(8,128)S(1)}, f32[4,48,128]{2,1,0:T(8,128)S(1)}, f3...) custom-call(s32[128,4096]{1,0:T(8,128)} %seqs_ref.1, f32[1088,512]{1,0:T(8,128)} %bitcast.5), custom_call_target="tpu_custom_call" | custom-call | tf_op jit(solution)/shard_map/logit_parts/pallas_call | solution.py:358
  4.6 3.3 %collective-permute-start = (f32[8,48,128]{2,1,0:T(8,128)S(1)}, f32[8,48,128]{2,1,0:T(8,128)S(1)}, u32[]{:S(2)}, u32[]{:S(2)}) collective-permute-start(f32[8,48,128]{2,1,0:T(8,128)S(1)} %get-tuple-element.25), channel_id=1, source_target_pairs={{0,8},{8,0},{16,24},{24,16},{32,40},{40,32},{48,56},{56,48},{64,72... | collective-permute-start | bytes 589832 | tf_op jit(solution)/shard_map/ppermute | solution.py:380
  8.0 0.0 collective-permute-start.1
  8.0 4.4 %collective-permute-done.1.got_ref = f32[4,48,128]{2,1,0:T(8,128)S(1)} collective-permute-done((f32[4,48,128]{2,1,0:T(8,128)S(1)}, f32[4,48,128]{2,1,0:T(8,128)S(1)}, u32[]{:S(2)}, u32[]{:S(2)}) %collective-permute-start.1) | collective-permute-done | bytes 98336 | tf_op jit(solution)/shard_map/ppermute | solution.py:32
  12.3 0.0 collective-permute-done.core_ref
  12.3 0.7 %combine.1 = (f32[8,48,128]{2,1,0:T(8,128)}, f32[48,128]{1,0:T(8,128)S(1)}, f32[48,128]{1,0:T(8,128)S(1)}, f32[48,128]{1,0:T(8,128)S(1)}, f32[48,128]{1,0:T(8,128)S(1)}, /*index=5*/f32[48,128]{1,0:T(8,128)S(1)}) custom-call(f32[8,48,128]{2,1,0:T(8,128)S(1)} %get-tuple-element.24.mine_ref, f32[8,48,128]{2,1,0:T(8,128)S(1)} %collective-permute-done.core_ref, ...), custom_call_target="tpu_custom_call" | custom-call | tf_op jit(solution)/shard_map/combine/pallas_call | solution.py:382
  13.0 7.1 %all-to-all-start = ((f32[8,48,128]{2,1,0:T(8,128)}), f32[8,48,128]{2,1,0:T(8,128)S(1)}, u32[]{:S(2)}, u32[]{:S(2)}) async-start(f32[8,48,128]{2,1,0:T(8,128)} %get-tuple-element.28), calls=%async_computation | async-start | bytes 393216 | tf_op jit(solution)/shard_map/all_to_all | solution.py:385
  20.2 2.7 %collective-permute-start.2 = (f32[48,128]{1,0:T(8,128)S(1)}, f32[48,128]{1,0:T(8,128)S(1)}, u32[]{:S(2)}, u32[]{:S(2)}) collective-permute-start(f32[48,128]{1,0:T(8,128)S(1)} %get-tuple-element.31), channel_id=1, source_target_pairs={{0,3},{1,2},{2,1},{3,0},{4,7},{5,6},{6,5},{7,4},{8,11},{9,10},{10,... | collective-permute-start | bytes 73736 | tf_op jit(solution)/shard_map/ppermute | solution.py:32
  22.9 0.3 collective-permute-start.3
  23.3 0.2 collective-permute-start.4
  23.5 0.3 flip.1
  23.8 0.6 %collective-permute-done.2.rest_0_ = f32[48,128]{1,0:T(8,128)S(1)} collective-permute-done((f32[48,128]{1,0:T(8,128)S(1)}, f32[48,128]{1,0:T(8,128)S(1)}, u32[]{:S(2)}, u32[]{:S(2)}) %collective-permute-start.2) | collective-permute-done | bytes 24608 | tf_op jit(solution)/shard_map/ppermute | solution.py:32
  24.4 2.9 %collective-permute-done.3.rest_1_ = f32[48,128]{1,0:T(8,128)S(1)} collective-permute-done((f32[48,128]{1,0:T(8,128)S(1)}, f32[48,128]{1,0:T(8,128)S(1)}, u32[]{:S(2)}, u32[]{:S(2)}) %collective-permute-start.3) | collective-permute-done | bytes 24608 | tf_op jit(solution)/shard_map/ppermute | solution.py:32
  27.4 0.0 collective-permute-done.4.rest_2_
  27.4 0.0 all-to-all-done.z_ref
  27.4 0.1 sum_parts.1.here_ref
  27.4 2.8 %collective-permute-start.5 = (f32[96,128]{1,0:T(8,128)S(1)}, f32[96,128]{1,0:T(8,128)S(1)}, u32[]{:S(2)}, u32[]{:S(2)}) collective-permute-start(f32[96,128]{1,0:T(8,128)S(1)} %sum_parts.1.here_ref), channel_id=1, source_target_pairs={{0,128},{8,136},{16,144},{24,152},{32,160},{40,168},{48,176},{56,1... | collective-permute-start | bytes 147464 | tf_op jit(solution)/shard_map/ppermute | solution.py:393
  30.3 1.7 %collective-permute-done.5.there_ref = f32[96,128]{1,0:T(8,128)S(1)} collective-permute-done((f32[96,128]{1,0:T(8,128)S(1)}, f32[96,128]{1,0:T(8,128)S(1)}, u32[]{:S(2)}, u32[]{:S(2)}) %collective-permute-start.5) | collective-permute-done | bytes 49184 | tf_op jit(solution)/shard_map/ppermute | solution.py:393
  32.0 0.8 %softmax.1 = (f32[8,48,128]{2,1,0:T(8,128)}, f32[48,128]{1,0:T(8,128)S(1)}, f32[48,128]{1,0:T(8,128)S(1)}, f32[1,128]{1,0:T(1,128)S(1)}) custom-call(f32[96,128]{1,0:T(8,128)S(1)} %sum_parts.1.here_ref, f32[96,128]{1,0:T(8,128)S(1)} %collective-permute-done.5.there_ref, f32[2,16,128]{2,1,0:T(8,128)S(1)} %get-tuple-element.35.codes_ref, f32[128,128]{1,0:T(8,128)S(1)} %bitcast.7), custom_call_target="tpu_custom_call" | custom-call | tf_op jit(solution)/shard_map/softmax/pallas_call | solution.py:394
  32.8 1.2 %collective-permute-start.6 = (f32[48,128]{1,0:T(8,128)S(1)}, f32[48,128]{1,0:T(8,128)S(1)}, u32[]{:S(2)}, u32[]{:S(2)}) collective-permute-start(f32[48,128]{1,0:T(8,128)S(1)} %get-tuple-element.36.own_ref), channel_id=1, source_target_pairs={{0,4},{1,5},{2,6},{3,7},{4,0},{5,1},{6,2},{7,3},{8,12},{9,13},{10,... | collective-permute-start | bytes 73736 | tf_op jit(solution)/shard_map/ppermute | solution.py:32
  34.0 6.4 %all-to-all-start.1 = ((f32[8,48,128]{2,1,0:T(8,128)}), f32[8,48,128]{2,1,0:T(8,128)S(1)}, u32[]{:S(2)}, u32[]{:S(2)}) async-start(f32[8,48,128]{2,1,0:T(8,128)} %get-tuple-element.37), calls=%async_computation.1 | async-start | bytes 393216 | tf_op jit(solution)/shard_map/all_to_all | solution.py:400
  40.4 0.0 collective-permute-done.6.got_ref
  40.4 1.9 %collective-permute-start.9 = (f32[2,48,128]{2,1,0:T(8,128)S(1)}, f32[2,48,128]{2,1,0:T(8,128)S(1)}, u32[]{:S(2)}, u32[]{:S(2)}) collective-permute-start(f32[2,48,128]{2,1,0:T(8,128)S(1)} %pair.1.rest_0_), channel_id=1, source_target_pairs={{0,3},{1,2},{2,1},{3,0},{4,7},{5,6},{6,5},{7,4},{8,11},{9,10},{10,... | collective-permute-start | bytes 147464 | tf_op jit(solution)/shard_map/ppermute | solution.py:32
  42.3 0.3 collective-permute-start.8
  42.7 1.1 %collective-permute-start.7 = (f32[2,48,128]{2,1,0:T(8,128)S(1)}, f32[2,48,128]{2,1,0:T(8,128)S(1)}, u32[]{:S(2)}, u32[]{:S(2)}) collective-permute-start(f32[2,48,128]{2,1,0:T(8,128)S(1)} %pair.1.rest_0_), channel_id=1, source_target_pairs={{0,1},{1,0},{2,3},{3,2},{4,5},{5,4},{6,7},{7,6},{8,9},{9,8},{10,11... | collective-permute-start | bytes 147464 | tf_op jit(solution)/shard_map/ppermute | solution.py:32
  43.8 2.5 %all-to-all-done.1.z_ref = f32[8,48,128]{2,1,0:T(8,128)S(1)} async-done(((f32[8,48,128]{2,1,0:T(8,128)}), f32[8,48,128]{2,1,0:T(8,128)S(1)}, u32[]{:S(2)}, u32[]{:S(2)}) %all-to-all-start.1) | async-done | bytes 196640 | tf_op jit(solution)/shard_map/all_to_all | solution.py:400
  46.3 5.6 %collective-permute-start.10 = (f32[8,48,128]{2,1,0:T(8,128)S(1)}, f32[8,48,128]{2,1,0:T(8,128)S(1)}, u32[]{:S(2)}, u32[]{:S(2)}) collective-permute-start(f32[8,48,128]{2,1,0:T(8,128)S(1)} %choose.1), channel_id=1, source_target_pairs={{0,8},{8,0},{16,24},{24,16},{32,40},{40,32},{48,56},{56,48},{64,72... | collective-permute-start | bytes 589832 | tf_op jit(solution)/shard_map/ppermute | solution.py:403
  51.9 0.5 slice_bitcast_fusion
  52.4 0.0 collective-permute-done.9.rest_3_
  52.5 0.0 collective-permute-done.8.rest_2_
  52.5 0.6 %update_rows.1.part_ref = f32[1088,512]{1,0:T(8,128)S(1)} custom-call(f32[1088,512]{1,0:T(8,128)S(1)} %bitcast.6, bf16[1088,128]{1,0:T(8,128)(2,1)S(1)} %get-tuple-element.23.hot_ref.hot_cols_ref, f32[2,48,128]{2,1,0:T(8,128)S(1)} %pair.1.rest_0_, f32[2,48,128]{2,1,0:T(8,128)S(1)} %collective-permute-done.7.rest_1_, ...), custom_call_target="tpu_custom_call" | custom-call | tf_op jit(solution)/shard_map/update_rows/pallas_call | solution.py:406
  53.1 1.7 %update_cols.1 = f32[1088,512]{1,0:T(8,128)} custom-call(f32[1088,512]{1,0:T(8,128)S(1)} %update_rows.1.part_ref, f32[8,48,128]{2,1,0:T(8,128)S(1)} %all-to-all-done.1.z_ref, f32[48,128]{1,0:T(8,128)S(1)} %get-tuple-element.38.other_ref, f32[8,48,128]{2,1,0:T(8,128)S(1)} %collective-permute-done.10.core_ref, bf16[128,512]{1,0:T(8,128)(2,1)S(1)} %get-tuple-element.30.hot_rows_ref), custom_call_target="tpu_custom_call" | custom-call | tf_op jit(solution)/shard_map/update_cols/pallas_call | solution.py:409
  (8 shorter events, 0.0 us)
Async XLA Ops:
  0.6 31.3 %copy-start.1 = (f32[16384]{0:T(1024)S(1)}, f32[16384]{0:T(1024)}, u32[]{:S(2)}) copy-start(f32[16384]{0:T(1024)} %param.4) | copy-start | bytes 196612
  4.6 7.7 %collective-permute-start = (f32[8,48,128]{2,1,0:T(8,128)S(1)}, f32[8,48,128]{2,1,0:T(8,128)S(1)}, u32[]{:S(2)}, u32[]{:S(2)}) collective-permute-start(f32[8,48,128]{2,1,0:T(8,128)S(1)} %get-tuple-element.25), channel_id=1, source_target_pairs={{0,8},{8,0},{16,24},{24,16},{32,40},{40,32},{48,56},{56,48},{64,72... | collective-permute-start | bytes 589832 | tf_op jit(solution)/shard_map/ppermute | solution.py:380
  8.0 4.4 %collective-permute-start.1 = (f32[4,48,128]{2,1,0:T(8,128)S(1)}, f32[4,48,128]{2,1,0:T(8,128)S(1)}, u32[]{:S(2)}, u32[]{:S(2)}) collective-permute-start(f32[4,48,128]{2,1,0:T(8,128)S(1)} %get-tuple-element.27), channel_id=1, source_target_pairs={{0,4},{1,5},{2,6},{3,7},{4,0},{5,1},{6,2},{7,3},{8,12},{9,13},{10,... | collective-permute-start | bytes 294920 | tf_op jit(solution)/shard_map/ppermute | solution.py:32
  13.0 14.3 %all-to-all-start = ((f32[8,48,128]{2,1,0:T(8,128)}), f32[8,48,128]{2,1,0:T(8,128)S(1)}, u32[]{:S(2)}, u32[]{:S(2)}) async-start(f32[8,48,128]{2,1,0:T(8,128)} %get-tuple-element.28), calls=%async_computation | async-start | bytes 393216 | tf_op jit(solution)/shard_map/all_to_all | solution.py:385
  20.2 4.3 %collective-permute-start.2 = (f32[48,128]{1,0:T(8,128)S(1)}, f32[48,128]{1,0:T(8,128)S(1)}, u32[]{:S(2)}, u32[]{:S(2)}) collective-permute-start(f32[48,128]{1,0:T(8,128)S(1)} %get-tuple-element.31), channel_id=1, source_target_pairs={{0,3},{1,2},{2,1},{3,0},{4,7},{5,6},{6,5},{7,4},{8,11},{9,10},{10,... | collective-permute-start | bytes 73736 | tf_op jit(solution)/shard_map/ppermute | solution.py:32
  22.9 4.4 %collective-permute-start.3 = (f32[48,128]{1,0:T(8,128)S(1)}, f32[48,128]{1,0:T(8,128)S(1)}, u32[]{:S(2)}, u32[]{:S(2)}) collective-permute-start(f32[48,128]{1,0:T(8,128)S(1)} %get-tuple-element.32), channel_id=1, source_target_pairs={{0,2},{1,3},{2,0},{3,1},{4,6},{5,7},{6,4},{7,5},{8,10},{9,11},{10,... | collective-permute-start | bytes 73736 | tf_op jit(solution)/shard_map/ppermute | solution.py:32
  23.3 4.1 %collective-permute-start.4 = (f32[48,128]{1,0:T(8,128)S(1)}, f32[48,128]{1,0:T(8,128)S(1)}, u32[]{:S(2)}, u32[]{:S(2)}) collective-permute-start(f32[48,128]{1,0:T(8,128)S(1)} %get-tuple-element.33), channel_id=1, source_target_pairs={{0,1},{1,0},{2,3},{3,2},{4,5},{5,4},{6,7},{7,6},{8,9},{9,8},{10,11... | collective-permute-start | bytes 73736 | tf_op jit(solution)/shard_map/ppermute | solution.py:32
  27.4 4.5 %collective-permute-start.5 = (f32[96,128]{1,0:T(8,128)S(1)}, f32[96,128]{1,0:T(8,128)S(1)}, u32[]{:S(2)}, u32[]{:S(2)}) collective-permute-start(f32[96,128]{1,0:T(8,128)S(1)} %sum_parts.1.here_ref), channel_id=1, source_target_pairs={{0,128},{8,136},{16,144},{24,152},{32,160},{40,168},{48,176},{56,1... | collective-permute-start | bytes 147464 | tf_op jit(solution)/shard_map/ppermute | solution.py:393
  32.8 7.6 %collective-permute-start.6 = (f32[48,128]{1,0:T(8,128)S(1)}, f32[48,128]{1,0:T(8,128)S(1)}, u32[]{:S(2)}, u32[]{:S(2)}) collective-permute-start(f32[48,128]{1,0:T(8,128)S(1)} %get-tuple-element.36.own_ref), channel_id=1, source_target_pairs={{0,4},{1,5},{2,6},{3,7},{4,0},{5,1},{6,2},{7,3},{8,12},{9,13},{10,... | collective-permute-start | bytes 73736 | tf_op jit(solution)/shard_map/ppermute | solution.py:32
  34.0 12.3 %all-to-all-start.1 = ((f32[8,48,128]{2,1,0:T(8,128)}), f32[8,48,128]{2,1,0:T(8,128)S(1)}, u32[]{:S(2)}, u32[]{:S(2)}) async-start(f32[8,48,128]{2,1,0:T(8,128)} %get-tuple-element.37), calls=%async_computation.1 | async-start | bytes 393216 | tf_op jit(solution)/shard_map/all_to_all | solution.py:400
  40.4 12.1 %copy-start = (f32[512,1088]{0,1:T(8,128)S(1)}, f32[512,1088]{0,1:T(8,128)}, u32[]{:S(2)}) copy-start(f32[512,1088]{0,1:T(8,128)} %param.5) | copy-start | bytes 6684676
  40.4 12.0 %collective-permute-start.9 = (f32[2,48,128]{2,1,0:T(8,128)S(1)}, f32[2,48,128]{2,1,0:T(8,128)S(1)}, u32[]{:S(2)}, u32[]{:S(2)}) collective-permute-start(f32[2,48,128]{2,1,0:T(8,128)S(1)} %pair.1.rest_0_), channel_id=1, source_target_pairs={{0,3},{1,2},{2,1},{3,0},{4,7},{5,6},{6,5},{7,4},{8,11},{9,10},{10,... | collective-permute-start | bytes 147464 | tf_op jit(solution)/shard_map/ppermute | solution.py:32
  42.3 10.1 %collective-permute-start.8 = (f32[2,48,128]{2,1,0:T(8,128)S(1)}, f32[2,48,128]{2,1,0:T(8,128)S(1)}, u32[]{:S(2)}, u32[]{:S(2)}) collective-permute-start(f32[2,48,128]{2,1,0:T(8,128)S(1)} %pair.1.rest_0_), channel_id=1, source_target_pairs={{0,2},{1,3},{2,0},{3,1},{4,6},{5,7},{6,4},{7,5},{8,10},{9,11},{10,... | collective-permute-start | bytes 147464 | tf_op jit(solution)/shard_map/ppermute | solution.py:32
  42.7 9.8 %collective-permute-start.7 = (f32[2,48,128]{2,1,0:T(8,128)S(1)}, f32[2,48,128]{2,1,0:T(8,128)S(1)}, u32[]{:S(2)}, u32[]{:S(2)}) collective-permute-start(f32[2,48,128]{2,1,0:T(8,128)S(1)} %pair.1.rest_0_), channel_id=1, source_target_pairs={{0,1},{1,0},{2,3},{3,2},{4,5},{5,4},{6,7},{7,6},{8,9},{9,8},{10,11... | collective-permute-start | bytes 147464 | tf_op jit(solution)/shard_map/ppermute | solution.py:32
  46.3 6.8 %collective-permute-start.10 = (f32[8,48,128]{2,1,0:T(8,128)S(1)}, f32[8,48,128]{2,1,0:T(8,128)S(1)}, u32[]{:S(2)}, u32[]{:S(2)}) collective-permute-start(f32[8,48,128]{2,1,0:T(8,128)S(1)} %choose.1), channel_id=1, source_target_pairs={{0,8},{8,0},{16,24},{24,16},{32,40},{40,32},{48,56},{56,48},{64,72... | collective-permute-start | bytes 589832 | tf_op jit(solution)/shard_map/ppermute | solution.py:403

commit v4 on v3

--- a/solution.py
+++ b/solution.py
@@ -22,8 +22,15 @@
 field_decay = 0.1
 
 DEPTH = 8
-PLANES = [7, 6, 5, 4, 0, 1, 2, 3]
-Z_GROUPS = [[(h * DEPTH + z) * 2 + k for z in PLANES] for h in range(2) for k in range(2)]
+FIRST = [4, 5, 6, 7, 0, 1, 2, 3]
+SECOND = [7, 6, 5, 4, 3, 2, 1, 0]
+
+
+def z_exchange(x, planes):
+    groups = [[(h * DEPTH + z) * 2 + k for z in planes] for h in range(2) for k in range(2)]
+    return lax.all_to_all(x, "row", 0, 0, tiled=True, axis_index_groups=groups)
+
+
 SWAP_CORES = [(i, i ^ 1) for i in range(ROWS)]
 SWAP_HALVES = [(i, i ^ HALF) for i in range(ROWS)]
 
@@ -144,9 +151,12 @@
             to[step % NEAR, place, :] = row_t[pl.ds(start + a, LOCI, stride=Q), :] - last
 
 
-def slot_of(z):
-    z = lax.rem(z, DEPTH)
-    return jnp.where(z < 4, z + 4, 7 - z)
+def first_slot(z):
+    return lax.rem(z + 4, DEPTH)
+
+
+def second_slot(z):
+    return 7 - lax.rem(z, DEPTH)
 
 
 def place_of():
@@ -163,7 +173,7 @@
         if d:
             value = value + mine_ref[d - 1]
         if d < DEPTH:
-            z_ref[slot_of(z_at + d)] = value
+            z_ref[first_slot(z_at + d)] = value
         else:
             last_ref[...] = value
     for step in range(NEAR):
@@ -179,7 +189,7 @@
         own = own + row_refs[step][...]
     other = last_ref[...]
     for s in range(DEPTH):
-        part = z_ref[PLANES.index(s)]
+        part = z_ref[FIRST.index(s)]
         own = own + jnp.where(s <= z_at, part, 0.0)
         other = other + jnp.where(s > z_at, part, 0.0)
     out_ref[:SENT, :] = own
@@ -189,8 +199,8 @@
 def choose_kernel(z_ref, other_ref, core_ref):
     _, odd, z_at = place_of()
     for e in range(DEPTH):
-        lower = z_ref[slot_of(z_at + e)]
-        upper = z_ref[slot_of(z_at + e + 1)] if e < DEPTH - 1 else other_ref[...]
+        lower = z_ref[second_slot(z_at + e)]
+        upper = z_ref[second_slot(z_at + e + 1)] if e < DEPTH - 1 else other_ref[...]
         core_ref[e] = jnp.where(odd, lower, upper)
 
 
@@ -261,7 +271,7 @@
         other_ref[place, :] = other[a]
         row_ref[place, :] = own[a]
         for s in range(DEPTH):
-            z_ref[PLANES.index(s), place, :] = jnp.where(z_at >= s, own[a], other[a])
+            z_ref[SECOND.index(s), place, :] = jnp.where(z_at >= s, own[a], other[a])
 
 
 def fill(part, to_ref, at):
@@ -301,7 +311,7 @@
         if j % 2:
             part = core_ref[j // 2]
         elif j < HALF:
-            part = z_ref[slot_of(z_at + j // 2)]
+            part = z_ref[second_slot(z_at + j // 2)]
         else:
             part = other_ref[...]
         fill(part, cols, j * PIECE)
@@ -382,7 +392,7 @@
     z_send, last, *parts = call(
         combine_kernel, (eight, piece) + (piece,) * NEAR, name="combine"
     )(mine, core, keep, give)
-    z_got = lax.all_to_all(z_send, "row", 0, 0, tiled=True, axis_index_groups=Z_GROUPS)
+    z_got = z_exchange(z_send, FIRST)
     row_got = [swap_cols(parts[step], step) for step in (3, 2, 1)] + [parts[0]]
     hot_cols, hot_rows = call(
         flip_kernel, (arr(BAND, BATCH, dtype=bf16), arr(BATCH, SPAN, dtype=bf16)), name="flip"
@@ -397,7 +407,7 @@
         name="softmax",
     )(here, there, codes, fields.reshape(-1, 128))
     across = swap_cols(resid, NEAR)
-    z_all = lax.all_to_all(z_send, "row", 0, 0, tiled=True, axis_index_groups=Z_GROUPS)
+    z_all = z_exchange(z_send, SECOND)
     pair = call(pair_kernel, arr(2, SENT, BATCH), name="pair", cost=COST)(resid, across)
     row_all = [pair] + [swap_cols(pair, step) for step in range(1, NEAR)]
     core_all = lax.ppermute(

time: 55.1 us -> 52.9 us (0.960)
  starting transfers between devices: 33.3 us -> 32 us
  waiting for transfers between devices: 12.1 us -> 11.2 us
    all_to_all x2, starting transfers between devices: 13.5 us -> 12.7 us  [z_exchange(): return lax.all_to_all(x, 'row', 0, 0, tiled=True, axis_index_groups=groups)]
    all_to_all x2, waiting for transfers between devices: 2.5 us -> 1.83 us  [z_exchange(): return lax.all_to_all(x, 'row', 0, 0, tiled=True, axis_index_groups=groups)]
where the time goes in v4:
time: 52.9 us; the launch traced here: 52.6 us
  starting transfers between devices  32 us (60%)
  waiting for transfers between devices  11.2 us (21%)
  Pallas kernels  8.2 us (16%)
  between operations  0.71 us (1%)
    all_to_all x2, starting transfers between devices, z_exchange(): return lax.all_to_all(x, 'row', 0, 0, tiled=True, axis_index_groups=groups)  12.7 us
    ppermute x8, starting transfers between devices, swap_cols(): return lax.ppermute(x, 'col', [(i, i ^ step) for i in range(COLS)])  7.87 us
    ppermute x8, waiting for transfers between devices, swap_cols(): return lax.ppermute(x, 'col', [(i, i ^ step) for i in range(COLS)])  7.63 us
    ppermute x1, starting transfers between devices, shards(): lax.ppermute(call(choose_kernel, eight, name='choose')(z_all, other), 'ro...  5.24 us
    pallas_call x1, Pallas kernels, shards(): call(logits_kernel, (arr(2, LOCI, BATCH), eight, eight, four, four, arr(B...  3.99 us
    ppermute x1, starting transfers between devices, shards(): core = lax.ppermute(core, 'row', SWAP_CORES)  3.33 us
    ppermute x1, starting transfers between devices, shards(): there = lax.ppermute(here, 'row', SWAP_HALVES)  2.83 us
    all_to_all x2, waiting for transfers between devices, z_exchange(): return lax.all_to_all(x, 'row', 0, 0, tiled=True, axis_index_groups=groups)  1.83 us
  transfers between devices with their start and end apart: 13, of which 5 were waited for; matrix products, arithmetic and copies ran while one was open for 1% of the time, Pallas kernels for 2%

profile of v4, /device:TPU:1, one launch (start us, length us, event | category | flops | bytes accessed | tf_op | source)
XLA Modules:
  0.0 52.6 jit_solution(18305513754117480383)
XLA Ops:
  0.6 4.0 %logit_parts.1 = (f32[2,16,128]{2,1,0:T(8,128)S(1)}, f32[8,48,128]{2,1,0:T(8,128)S(1)}, f32[8,48,128]{2,1,0:T(8,128)S(1)}, f32[4,48,128]{2,1,0:T(8,128)S(1)}, f3...) custom-call(s32[128,4096]{1,0:T(8,128)} %seqs_ref.1, f32[1088,512]{1,0:T(8,128)} %bitcast.5), custom_call_target="tpu_custom_call" | custom-call | tf_op jit(solution)/shard_map/logit_parts/pallas_call | solution.py:368
  4.6 3.3 %collective-permute-start = (f32[8,48,128]{2,1,0:T(8,128)S(1)}, f32[8,48,128]{2,1,0:T(8,128)S(1)}, u32[]{:S(2)}, u32[]{:S(2)}) collective-permute-start(f32[8,48,128]{2,1,0:T(8,128)S(1)} %get-tuple-element.25), channel_id=1, source_target_pairs={{0,8},{8,0},{16,24},{24,16},{32,40},{40,32},{48,56},{56,48},{64,72... | collective-permute-start | bytes 589832 | tf_op jit(solution)/shard_map/ppermute | solution.py:390
  8.0 0.0 collective-permute-start.1
  8.0 4.4 %collective-permute-done.1.got_ref = f32[4,48,128]{2,1,0:T(8,128)S(1)} collective-permute-done((f32[4,48,128]{2,1,0:T(8,128)S(1)}, f32[4,48,128]{2,1,0:T(8,128)S(1)}, u32[]{:S(2)}, u32[]{:S(2)}) %collective-permute-start.1) | collective-permute-done | bytes 98336 | tf_op jit(solution)/shard_map/ppermute | solution.py:39
  12.3 0.0 collective-permute-done.core_ref
  12.3 0.7 %combine.1 = (f32[8,48,128]{2,1,0:T(8,128)}, f32[48,128]{1,0:T(8,128)S(1)}, f32[48,128]{1,0:T(8,128)S(1)}, f32[48,128]{1,0:T(8,128)S(1)}, f32[48,128]{1,0:T(8,128)S(1)}, /*index=5*/f32[48,128]{1,0:T(8,128)S(1)}) custom-call(f32[8,48,128]{2,1,0:T(8,128)S(1)} %get-tuple-element.24.mine_ref, f32[8,48,128]{2,1,0:T(8,128)S(1)} %collective-permute-done.core_ref, ...), custom_call_target="tpu_custom_call" | custom-call | tf_op jit(solution)/shard_map/combine/pallas_call | solution.py:392
  13.0 8.5 %all-to-all-start = ((f32[8,48,128]{2,1,0:T(8,128)}), f32[8,48,128]{2,1,0:T(8,128)S(1)}, u32[]{:S(2)}, u32[]{:S(2)}) async-start(f32[8,48,128]{2,1,0:T(8,128)} %get-tuple-element.28), calls=%async_computation | async-start | bytes 393216 | tf_op jit(solution)/shard_map/all_to_all | solution.py:31
  21.5 2.7 %collective-permute-start.2 = (f32[48,128]{1,0:T(8,128)S(1)}, f32[48,128]{1,0:T(8,128)S(1)}, u32[]{:S(2)}, u32[]{:S(2)}) collective-permute-start(f32[48,128]{1,0:T(8,128)S(1)} %get-tuple-element.31), channel_id=1, source_target_pairs={{0,3},{1,2},{2,1},{3,0},{4,7},{5,6},{6,5},{7,4},{8,11},{9,10},{10,... | collective-permute-start | bytes 73736 | tf_op jit(solution)/shard_map/ppermute | solution.py:39
  24.3 0.3 collective-permute-start.3
  24.6 0.2 collective-permute-start.4
  24.8 0.3 flip.1
  25.2 0.4 collective-permute-done.2.rest_0_
  25.6 2.8 %collective-permute-done.3.rest_1_ = f32[48,128]{1,0:T(8,128)S(1)} collective-permute-done((f32[48,128]{1,0:T(8,128)S(1)}, f32[48,128]{1,0:T(8,128)S(1)}, u32[]{:S(2)}, u32[]{:S(2)}) %collective-permute-start.3) | collective-permute-done | bytes 24608 | tf_op jit(solution)/shard_map/ppermute | solution.py:39
  28.4 0.0 collective-permute-done.4.rest_2_
  28.5 0.1 sum_parts.1.here_ref
  28.5 2.8 %collective-permute-start.5 = (f32[96,128]{1,0:T(8,128)S(1)}, f32[96,128]{1,0:T(8,128)S(1)}, u32[]{:S(2)}, u32[]{:S(2)}) collective-permute-start(f32[96,128]{1,0:T(8,128)S(1)} %sum_parts.1.here_ref), channel_id=1, source_target_pairs={{0,128},{8,136},{16,144},{24,152},{32,160},{40,168},{48,176},{56,1... | collective-permute-start | bytes 147464 | tf_op jit(solution)/shard_map/ppermute | solution.py:403
  31.3 1.7 %collective-permute-done.5.there_ref = f32[96,128]{1,0:T(8,128)S(1)} collective-permute-done((f32[96,128]{1,0:T(8,128)S(1)}, f32[96,128]{1,0:T(8,128)S(1)}, u32[]{:S(2)}, u32[]{:S(2)}) %collective-permute-start.5) | collective-permute-done | bytes 49184 | tf_op jit(solution)/shard_map/ppermute | solution.py:403
  33.0 0.8 %softmax.1 = (f32[8,48,128]{2,1,0:T(8,128)}, f32[48,128]{1,0:T(8,128)S(1)}, f32[48,128]{1,0:T(8,128)S(1)}, f32[1,128]{1,0:T(1,128)S(1)}) custom-call(f32[96,128]{1,0:T(8,128)S(1)} %sum_parts.1.here_ref, f32[96,128]{1,0:T(8,128)S(1)} %collective-permute-done.5.there_ref, f32[2,16,128]{2,1,0:T(8,128)S(1)} %get-tuple-element.35.codes_ref, f32[128,128]{1,0:T(8,128)S(1)} %bitcast.7), custom_call_target="tpu_custom_call" | custom-call | tf_op jit(solution)/shard_map/softmax/pallas_call | solution.py:404
  33.9 1.2 %collective-permute-start.6 = (f32[48,128]{1,0:T(8,128)S(1)}, f32[48,128]{1,0:T(8,128)S(1)}, u32[]{:S(2)}, u32[]{:S(2)}) collective-permute-start(f32[48,128]{1,0:T(8,128)S(1)} %get-tuple-element.36.own_ref), channel_id=1, source_target_pairs={{0,4},{1,5},{2,6},{3,7},{4,0},{5,1},{6,2},{7,3},{8,12},{9,13},{10,... | collective-permute-start | bytes 73736 | tf_op jit(solution)/shard_map/ppermute | solution.py:39
  35.1 4.3 %all-to-all-start.1 = ((f32[8,48,128]{2,1,0:T(8,128)}), f32[8,48,128]{2,1,0:T(8,128)S(1)}, u32[]{:S(2)}, u32[]{:S(2)}) async-start(f32[8,48,128]{2,1,0:T(8,128)} %get-tuple-element.37), calls=%async_computation.1 | async-start | bytes 393216 | tf_op jit(solution)/shard_map/all_to_all | solution.py:31
  39.4 2.2 %collective-permute-start.9 = (f32[2,48,128]{2,1,0:T(8,128)S(1)}, f32[2,48,128]{2,1,0:T(8,128)S(1)}, u32[]{:S(2)}, u32[]{:S(2)}) collective-permute-start(f32[2,48,128]{2,1,0:T(8,128)S(1)} %pair.1.rest_0_), channel_id=1, source_target_pairs={{0,3},{1,2},{2,1},{3,0},{4,7},{5,6},{6,5},{7,4},{8,11},{9,10},{10,... | collective-permute-start | bytes 147464 | tf_op jit(solution)/shard_map/ppermute | solution.py:39
  41.6 0.4 collective-permute-start.8
  42.0 0.7 %collective-permute-start.7 = (f32[2,48,128]{2,1,0:T(8,128)S(1)}, f32[2,48,128]{2,1,0:T(8,128)S(1)}, u32[]{:S(2)}, u32[]{:S(2)}) collective-permute-start(f32[2,48,128]{2,1,0:T(8,128)S(1)} %pair.1.rest_0_), channel_id=1, source_target_pairs={{0,1},{1,0},{2,3},{3,2},{4,5},{5,4},{6,7},{7,6},{8,9},{9,8},{10,11... | collective-permute-start | bytes 147464 | tf_op jit(solution)/shard_map/ppermute | solution.py:39
  42.7 1.8 %all-to-all-done.1.z_ref = f32[8,48,128]{2,1,0:T(8,128)S(1)} async-done(((f32[8,48,128]{2,1,0:T(8,128)}), f32[8,48,128]{2,1,0:T(8,128)S(1)}, u32[]{:S(2)}, u32[]{:S(2)}) %all-to-all-start.1) | async-done | bytes 196640 | tf_op jit(solution)/shard_map/all_to_all | solution.py:31
  44.5 5.2 %collective-permute-start.10 = (f32[8,48,128]{2,1,0:T(8,128)S(1)}, f32[8,48,128]{2,1,0:T(8,128)S(1)}, u32[]{:S(2)}, u32[]{:S(2)}) collective-permute-start(f32[8,48,128]{2,1,0:T(8,128)S(1)} %choose.1), channel_id=1, source_target_pairs={{0,8},{8,0},{16,24},{24,16},{32,40},{40,32},{48,56},{56,48},{64,72... | collective-permute-start | bytes 589832 | tf_op jit(solution)/shard_map/ppermute | solution.py:413
  49.8 0.5 slice_bitcast_fusion
  50.3 0.0 collective-permute-done.9.rest_3_
  50.3 0.0 collective-permute-done.8.rest_2_
  50.3 0.0 collective-permute-done.7.rest_1_
  50.3 0.6 %update_rows.1.part_ref = f32[1088,512]{1,0:T(8,128)S(1)} custom-call(f32[1088,512]{1,0:T(8,128)S(1)} %bitcast.6, bf16[1088,128]{1,0:T(8,128)(2,1)S(1)} %get-tuple-element.23.hot_ref.hot_cols_ref, f32[2,48,128]{2,1,0:T(8,128)S(1)} %pair.1.rest_0_, f32[2,48,128]{2,1,0:T(8,128)S(1)} %collective-permute-done.7.rest_1_, ...), custom_call_target="tpu_custom_call" | custom-call | tf_op jit(solution)/shard_map/update_rows/pallas_call | solution.py:416
  50.9 0.0 collective-permute-done.10.core_ref
  50.9 1.7 %update_cols.1 = f32[1088,512]{1,0:T(8,128)} custom-call(f32[1088,512]{1,0:T(8,128)S(1)} %update_rows.1.part_ref, f32[8,48,128]{2,1,0:T(8,128)S(1)} %all-to-all-done.1.z_ref, f32[48,128]{1,0:T(8,128)S(1)} %get-tuple-element.38.other_ref, f32[8,48,128]{2,1,0:T(8,128)S(1)} %collective-permute-done.10.core_ref, bf16[128,512]{1,0:T(8,128)(2,1)S(1)} %get-tuple-element.30.hot_rows_ref), custom_call_target="tpu_custom_call" | custom-call | tf_op jit(solution)/shard_map/update_cols/pallas_call | solution.py:419
  (8 shorter events, 0.0 us)
Async XLA Ops:
  0.6 32.4 %copy-start.1 = (f32[16384]{0:T(1024)S(1)}, f32[16384]{0:T(1024)}, u32[]{:S(2)}) copy-start(f32[16384]{0:T(1024)} %param.4) | copy-start | bytes 196612
  4.6 7.7 %collective-permute-start = (f32[8,48,128]{2,1,0:T(8,128)S(1)}, f32[8,48,128]{2,1,0:T(8,128)S(1)}, u32[]{:S(2)}, u32[]{:S(2)}) collective-permute-start(f32[8,48,128]{2,1,0:T(8,128)S(1)} %get-tuple-element.25), channel_id=1, source_target_pairs={{0,8},{8,0},{16,24},{24,16},{32,40},{40,32},{48,56},{56,48},{64,72... | collective-permute-start | bytes 589832 | tf_op jit(solution)/shard_map/ppermute | solution.py:390
  8.0 4.4 %collective-permute-start.1 = (f32[4,48,128]{2,1,0:T(8,128)S(1)}, f32[4,48,128]{2,1,0:T(8,128)S(1)}, u32[]{:S(2)}, u32[]{:S(2)}) collective-permute-start(f32[4,48,128]{2,1,0:T(8,128)S(1)} %get-tuple-element.27), channel_id=1, source_target_pairs={{0,4},{1,5},{2,6},{3,7},{4,0},{5,1},{6,2},{7,3},{8,12},{9,13},{10,... | collective-permute-start | bytes 294920 | tf_op jit(solution)/shard_map/ppermute | solution.py:39
  13.0 15.4 %all-to-all-start = ((f32[8,48,128]{2,1,0:T(8,128)}), f32[8,48,128]{2,1,0:T(8,128)S(1)}, u32[]{:S(2)}, u32[]{:S(2)}) async-start(f32[8,48,128]{2,1,0:T(8,128)} %get-tuple-element.28), calls=%async_computation | async-start | bytes 393216 | tf_op jit(solution)/shard_map/all_to_all | solution.py:31
  21.5 4.1 %collective-permute-start.2 = (f32[48,128]{1,0:T(8,128)S(1)}, f32[48,128]{1,0:T(8,128)S(1)}, u32[]{:S(2)}, u32[]{:S(2)}) collective-permute-start(f32[48,128]{1,0:T(8,128)S(1)} %get-tuple-element.31), channel_id=1, source_target_pairs={{0,3},{1,2},{2,1},{3,0},{4,7},{5,6},{6,5},{7,4},{8,11},{9,10},{10,... | collective-permute-start | bytes 73736 | tf_op jit(solution)/shard_map/ppermute | solution.py:39
  24.3 4.2 %collective-permute-start.3 = (f32[48,128]{1,0:T(8,128)S(1)}, f32[48,128]{1,0:T(8,128)S(1)}, u32[]{:S(2)}, u32[]{:S(2)}) collective-permute-start(f32[48,128]{1,0:T(8,128)S(1)} %get-tuple-element.32), channel_id=1, source_target_pairs={{0,2},{1,3},{2,0},{3,1},{4,6},{5,7},{6,4},{7,5},{8,10},{9,11},{10,... | collective-permute-start | bytes 73736 | tf_op jit(solution)/shard_map/ppermute | solution.py:39
  24.6 3.8 %collective-permute-start.4 = (f32[48,128]{1,0:T(8,128)S(1)}, f32[48,128]{1,0:T(8,128)S(1)}, u32[]{:S(2)}, u32[]{:S(2)}) collective-permute-start(f32[48,128]{1,0:T(8,128)S(1)} %get-tuple-element.33), channel_id=1, source_target_pairs={{0,1},{1,0},{2,3},{3,2},{4,5},{5,4},{6,7},{7,6},{8,9},{9,8},{10,11... | collective-permute-start | bytes 73736 | tf_op jit(solution)/shard_map/ppermute | solution.py:39
  28.5 4.5 %collective-permute-start.5 = (f32[96,128]{1,0:T(8,128)S(1)}, f32[96,128]{1,0:T(8,128)S(1)}, u32[]{:S(2)}, u32[]{:S(2)}) collective-permute-start(f32[96,128]{1,0:T(8,128)S(1)} %sum_parts.1.here_ref), channel_id=1, source_target_pairs={{0,128},{8,136},{16,144},{24,152},{32,160},{40,168},{48,176},{56,1... | collective-permute-start | bytes 147464 | tf_op jit(solution)/shard_map/ppermute | solution.py:403
  33.9 5.5 %collective-permute-start.6 = (f32[48,128]{1,0:T(8,128)S(1)}, f32[48,128]{1,0:T(8,128)S(1)}, u32[]{:S(2)}, u32[]{:S(2)}) collective-permute-start(f32[48,128]{1,0:T(8,128)S(1)} %get-tuple-element.36.own_ref), channel_id=1, source_target_pairs={{0,4},{1,5},{2,6},{3,7},{4,0},{5,1},{6,2},{7,3},{8,12},{9,13},{10,... | collective-permute-start | bytes 73736 | tf_op jit(solution)/shard_map/ppermute | solution.py:39
  35.1 9.4 %all-to-all-start.1 = ((f32[8,48,128]{2,1,0:T(8,128)}), f32[8,48,128]{2,1,0:T(8,128)S(1)}, u32[]{:S(2)}, u32[]{:S(2)}) async-start(f32[8,48,128]{2,1,0:T(8,128)} %get-tuple-element.37), calls=%async_computation.1 | async-start | bytes 393216 | tf_op jit(solution)/shard_map/all_to_all | solution.py:31
  39.3 11.0 %copy-start = (f32[512,1088]{0,1:T(8,128)S(1)}, f32[512,1088]{0,1:T(8,128)}, u32[]{:S(2)}) copy-start(f32[512,1088]{0,1:T(8,128)} %param.5) | copy-start | bytes 6684676
  39.4 10.9 %collective-permute-start.9 = (f32[2,48,128]{2,1,0:T(8,128)S(1)}, f32[2,48,128]{2,1,0:T(8,128)S(1)}, u32[]{:S(2)}, u32[]{:S(2)}) collective-permute-start(f32[2,48,128]{2,1,0:T(8,128)S(1)} %pair.1.rest_0_), channel_id=1, source_target_pairs={{0,3},{1,2},{2,1},{3,0},{4,7},{5,6},{6,5},{7,4},{8,11},{9,10},{10,... | collective-permute-start | bytes 147464 | tf_op jit(solution)/shard_map/ppermute | solution.py:39
  41.6 8.7 %collective-permute-start.8 = (f32[2,48,128]{2,1,0:T(8,128)S(1)}, f32[2,48,128]{2,1,0:T(8,128)S(1)}, u32[]{:S(2)}, u32[]{:S(2)}) collective-permute-start(f32[2,48,128]{2,1,0:T(8,128)S(1)} %pair.1.rest_0_), channel_id=1, source_target_pairs={{0,2},{1,3},{2,0},{3,1},{4,6},{5,7},{6,4},{7,5},{8,10},{9,11},{10,... | collective-permute-start | bytes 147464 | tf_op jit(solution)/shard_map/ppermute | solution.py:39
  42.0 8.3 %collective-permute-start.7 = (f32[2,48,128]{2,1,0:T(8,128)S(1)}, f32[2,48,128]{2,1,0:T(8,128)S(1)}, u32[]{:S(2)}, u32[]{:S(2)}) collective-permute-start(f32[2,48,128]{2,1,0:T(8,128)S(1)} %pair.1.rest_0_), channel_id=1, source_target_pairs={{0,1},{1,0},{2,3},{3,2},{4,5},{5,4},{6,7},{7,6},{8,9},{9,8},{10,11... | collective-permute-start | bytes 147464 | tf_op jit(solution)/shard_map/ppermute | solution.py:39
  44.5 6.4 %collective-permute-start.10 = (f32[8,48,128]{2,1,0:T(8,128)S(1)}, f32[8,48,128]{2,1,0:T(8,128)S(1)}, u32[]{:S(2)}, u32[]{:S(2)}) collective-permute-start(f32[8,48,128]{2,1,0:T(8,128)S(1)} %choose.1), channel_id=1, source_target_pairs={{0,8},{8,0},{16,24},{24,16},{32,40},{40,32},{48,56},{56,48},{64,72... | collective-permute-start | bytes 589832 | tf_op jit(solution)/shard_map/ppermute | solution.py:413

commit v5 on v4

--- a/solution.py
+++ b/solution.py
@@ -164,7 +164,7 @@
     return row_at, lax.rem(row_at, 2) == 1, lax.rem(row_at // 2, DEPTH)
 
 
-def combine_kernel(mine_ref, core_ref, keep_ref, got_ref, z_ref, last_ref, *part_refs):
+def combine_kernel(mine_ref, core_ref, z_ref, last_ref):
     _, odd, z_at = place_of()
     for d in range(DEPTH + 1):
         lower = core_ref[d] if d < DEPTH else jnp.zeros((SENT, BATCH), f32)
@@ -176,6 +176,10 @@
             z_ref[first_slot(z_at + d)] = value
         else:
             last_ref[...] = value
+
+
+def add_kernel(keep_ref, got_ref, last_ref, *part_refs):
+    del last_ref
     for step in range(NEAR):
         part_refs[step][...] = keep_ref[step] + got_ref[step]
 
@@ -389,9 +393,10 @@
     )(seqs, band_t)
     core = lax.ppermute(core, "row", SWAP_CORES)
     give = swap_cols(give, NEAR)
-    z_send, last, *parts = call(
-        combine_kernel, (eight, piece) + (piece,) * NEAR, name="combine"
-    )(mine, core, keep, give)
+    z_send, last = call(combine_kernel, (eight, piece), name="combine")(mine, core)
+    parts = call(add_kernel, (piece,) * NEAR, name="add_halves", cost=COST, loose=(2,), inputs=3)(
+        keep, give, last
+    )
     z_got = z_exchange(z_send, FIRST)
     row_got = [swap_cols(parts[step], step) for step in (3, 2, 1)] + [parts[0]]
     hot_cols, hot_rows = call(

time: 52.9 us -> 49.4 us (0.934)
  waiting for transfers between devices: 11.2 us -> 7.89 us
    ppermute x8, waiting for transfers between devices: 7.63 us -> 3.18 us  [swap_cols(): return lax.ppermute(x, 'col', [(i, i ^ step) for i in range(COLS)])]
    ppermute x1, waiting for transfers between devices: 0.01 us -> 1.07 us  [shards(): core = lax.ppermute(core, 'row', SWAP_CORES)]
    ppermute x1, starting transfers between devices: 5.24 us -> 4.56 us  [shards(): lax.ppermute(call(choose_kernel, eight, name='choose')(z_all, other), 'ro...]
  transfers between devices with their start and end apart: 13 -> 13, of which waited for: 5 -> 5; matrix products, arithmetic and copies ran while one was open for 1% -> 1% of each run, Pallas kernels for 2% -> 3%
where the time goes in v5:
time: 49.4 us; the launch traced here: 49.1 us
  starting transfers between devices  31.8 us (64%)
  Pallas kernels  8.18 us (17%)
  waiting for transfers between devices  7.89 us (16%)
  between operations  0.72 us (1%)
  local copies, waits for them, and re-layouts  0.52 us (1%)
    all_to_all x2, starting transfers between devices, z_exchange(): return lax.all_to_all(x, 'row', 0, 0, tiled=True, axis_index_groups=groups)  13.3 us
    ppermute x8, starting transfers between devices, swap_cols(): return lax.ppermute(x, 'col', [(i, i ^ step) for i in range(COLS)])  8.03 us
    ppermute x1, starting transfers between devices, shards(): lax.ppermute(call(choose_kernel, eight, name='choose')(z_all, other), 'ro...  4.56 us
    pallas_call x1, Pallas kernels, shards(): call(logits_kernel, (arr(2, LOCI, BATCH), eight, eight, four, four, arr(B...  3.96 us
    ppermute x1, starting transfers between devices, shards(): core = lax.ppermute(core, 'row', SWAP_CORES)  3.33 us
    ppermute x8, waiting for transfers between devices, swap_cols(): return lax.ppermute(x, 'col', [(i, i ^ step) for i in range(COLS)])  3.18 us
    ppermute x1, starting transfers between devices, shards(): there = lax.ppermute(here, 'row', SWAP_HALVES)  2.67 us
    ppermute x1, waiting for transfers between devices, shards(): there = lax.ppermute(here, 'row', SWAP_HALVES)  1.86 us
  transfers between devices with their start and end apart: 13, of which 5 were waited for; matrix products, arithmetic and copies ran while one was open for 1% of the time, Pallas kernels for 3%

profile of v5, /device:TPU:1, one launch (start us, length us, event | category | flops | bytes accessed | tf_op | source)
XLA Modules:
  0.0 49.1 jit_solution(7690921748198445673)
XLA Ops:
  0.6 4.0 %logit_parts.1 = (f32[2,16,128]{2,1,0:T(8,128)S(1)}, f32[8,48,128]{2,1,0:T(8,128)S(1)}, f32[8,48,128]{2,1,0:T(8,128)S(1)}, f32[4,48,128]{2,1,0:T(8,128)S(1)}, f3...) custom-call(s32[128,4096]{1,0:T(8,128)} %seqs_ref.1, f32[1088,512]{1,0:T(8,128)} %bitcast.5), custom_call_target="tpu_custom_call" | custom-call | tf_op jit(solution)/shard_map/logit_parts/pallas_call | solution.py:372
  4.6 3.3 %collective-permute-start = (f32[8,48,128]{2,1,0:T(8,128)S(1)}, f32[8,48,128]{2,1,0:T(8,128)S(1)}, u32[]{:S(2)}, u32[]{:S(2)}) collective-permute-start(f32[8,48,128]{2,1,0:T(8,128)S(1)} %get-tuple-element.25), channel_id=1, source_target_pairs={{0,8},{8,0},{16,24},{24,16},{32,40},{40,32},{48,56},{56,48},{64,72... | collective-permute-start | bytes 589832 | tf_op jit(solution)/shard_map/ppermute | solution.py:394
  7.9 0.0 collective-permute-start.1
  7.9 1.1 %collective-permute-done.core_ref = f32[8,48,128]{2,1,0:T(8,128)S(1)} collective-permute-done((f32[8,48,128]{2,1,0:T(8,128)S(1)}, f32[8,48,128]{2,1,0:T(8,128)S(1)}, u32[]{:S(2)}, u32[]{:S(2)}) %collective-permute-start) | collective-permute-done | bytes 196640 | tf_op jit(solution)/shard_map/ppermute | solution.py:394
  9.0 0.7 %combine.1 = (f32[8,48,128]{2,1,0:T(8,128)}, f32[48,128]{1,0:T(8,128)S(1)}) custom-call(f32[8,48,128]{2,1,0:T(8,128)S(1)} %get-tuple-element.24.mine_ref, f32[8,48,128]{2,1,0:T(8,128)S(1)} %collective-permute-done.core_ref), custom_call_target="tpu_custom_call" | custom-call | tf_op jit(solution)/shard_map/combine/pallas_call | solution.py:396
  9.7 8.7 %all-to-all-start = ((f32[8,48,128]{2,1,0:T(8,128)}), f32[8,48,128]{2,1,0:T(8,128)S(1)}, u32[]{:S(2)}, u32[]{:S(2)}) async-start(f32[8,48,128]{2,1,0:T(8,128)} %get-tuple-element.26), calls=%async_computation | async-start | bytes 393216 | tf_op jit(solution)/shard_map/all_to_all | solution.py:31
  18.4 0.0 collective-permute-done.1.got_ref
  18.4 2.8 %collective-permute-start.2 = (f32[48,128]{1,0:T(8,128)S(1)}, f32[48,128]{1,0:T(8,128)S(1)}, u32[]{:S(2)}, u32[]{:S(2)}) collective-permute-start(f32[48,128]{1,0:T(8,128)S(1)} %get-tuple-element.31), channel_id=1, source_target_pairs={{0,3},{1,2},{2,1},{3,0},{4,7},{5,6},{6,5},{7,4},{8,11},{9,10},{10,... | collective-permute-start | bytes 73736 | tf_op jit(solution)/shard_map/ppermute | solution.py:39
  21.2 0.4 collective-permute-start.3
  21.6 0.3 collective-permute-start.4
  21.9 0.3 flip.1
  22.2 0.5 %collective-permute-done.2.rest_0_ = f32[48,128]{1,0:T(8,128)S(1)} collective-permute-done((f32[48,128]{1,0:T(8,128)S(1)}, f32[48,128]{1,0:T(8,128)S(1)}, u32[]{:S(2)}, u32[]{:S(2)}) %collective-permute-start.2) | collective-permute-done | bytes 24608 | tf_op jit(solution)/shard_map/ppermute | solution.py:39
  22.7 2.7 %collective-permute-done.3.rest_1_ = f32[48,128]{1,0:T(8,128)S(1)} collective-permute-done((f32[48,128]{1,0:T(8,128)S(1)}, f32[48,128]{1,0:T(8,128)S(1)}, u32[]{:S(2)}, u32[]{:S(2)}) %collective-permute-start.3) | collective-permute-done | bytes 24608 | tf_op jit(solution)/shard_map/ppermute | solution.py:39
  25.4 0.0 collective-permute-done.4.rest_2_
  25.4 0.0 all-to-all-done.z_ref
  25.4 0.1 sum_parts.1.here_ref
  25.5 2.7 %collective-permute-start.5 = (f32[96,128]{1,0:T(8,128)S(1)}, f32[96,128]{1,0:T(8,128)S(1)}, u32[]{:S(2)}, u32[]{:S(2)}) collective-permute-start(f32[96,128]{1,0:T(8,128)S(1)} %sum_parts.1.here_ref), channel_id=1, source_target_pairs={{0,128},{8,136},{16,144},{24,152},{32,160},{40,168},{48,176},{56,1... | collective-permute-start | bytes 147464 | tf_op jit(solution)/shard_map/ppermute | solution.py:408
  28.1 1.9 %collective-permute-done.5.there_ref = f32[96,128]{1,0:T(8,128)S(1)} collective-permute-done((f32[96,128]{1,0:T(8,128)S(1)}, f32[96,128]{1,0:T(8,128)S(1)}, u32[]{:S(2)}, u32[]{:S(2)}) %collective-permute-start.5) | collective-permute-done | bytes 49184 | tf_op jit(solution)/shard_map/ppermute | solution.py:408
  30.0 0.8 %softmax.1 = (f32[8,48,128]{2,1,0:T(8,128)}, f32[48,128]{1,0:T(8,128)S(1)}, f32[48,128]{1,0:T(8,128)S(1)}, f32[1,128]{1,0:T(1,128)S(1)}) custom-call(f32[96,128]{1,0:T(8,128)S(1)} %sum_parts.1.here_ref, f32[96,128]{1,0:T(8,128)S(1)} %collective-permute-done.5.there_ref, f32[2,16,128]{2,1,0:T(8,128)S(1)} %get-tuple-element.35.codes_ref, f32[128,128]{1,0:T(8,128)S(1)} %bitcast.7), custom_call_target="tpu_custom_call" | custom-call | tf_op jit(solution)/shard_map/softmax/pallas_call | solution.py:409
  30.8 1.0 %collective-permute-start.6 = (f32[48,128]{1,0:T(8,128)S(1)}, f32[48,128]{1,0:T(8,128)S(1)}, u32[]{:S(2)}, u32[]{:S(2)}) collective-permute-start(f32[48,128]{1,0:T(8,128)S(1)} %get-tuple-element.36.own_ref), channel_id=1, source_target_pairs={{0,4},{1,5},{2,6},{3,7},{4,0},{5,1},{6,2},{7,3},{8,12},{9,13},{10,... | collective-permute-start | bytes 73736 | tf_op jit(solution)/shard_map/ppermute | solution.py:39
  31.9 4.6 %all-to-all-start.1 = ((f32[8,48,128]{2,1,0:T(8,128)}), f32[8,48,128]{2,1,0:T(8,128)S(1)}, u32[]{:S(2)}, u32[]{:S(2)}) async-start(f32[8,48,128]{2,1,0:T(8,128)} %get-tuple-element.37), calls=%async_computation.1 | async-start | bytes 393216 | tf_op jit(solution)/shard_map/all_to_all | solution.py:31
  36.4 0.0 collective-permute-done.6.got_ref
  36.5 2.8 %collective-permute-start.9 = (f32[2,48,128]{2,1,0:T(8,128)S(1)}, f32[2,48,128]{2,1,0:T(8,128)S(1)}, u32[]{:S(2)}, u32[]{:S(2)}) collective-permute-start(f32[2,48,128]{2,1,0:T(8,128)S(1)} %pair.1.rest_0_), channel_id=1, source_target_pairs={{0,3},{1,2},{2,1},{3,0},{4,7},{5,6},{6,5},{7,4},{8,11},{9,10},{10,... | collective-permute-start | bytes 147464 | tf_op jit(solution)/shard_map/ppermute | solution.py:39
  39.3 0.4 collective-permute-start.8
  39.6 0.3 collective-permute-start.7
  40.0 1.8 %all-to-all-done.1.z_ref = f32[8,48,128]{2,1,0:T(8,128)S(1)} async-done(((f32[8,48,128]{2,1,0:T(8,128)}), f32[8,48,128]{2,1,0:T(8,128)S(1)}, u32[]{:S(2)}, u32[]{:S(2)}) %all-to-all-start.1) | async-done | bytes 196640 | tf_op jit(solution)/shard_map/all_to_all | solution.py:31
  41.8 4.6 %collective-permute-start.10 = (f32[8,48,128]{2,1,0:T(8,128)S(1)}, f32[8,48,128]{2,1,0:T(8,128)S(1)}, u32[]{:S(2)}, u32[]{:S(2)}) collective-permute-start(f32[8,48,128]{2,1,0:T(8,128)S(1)} %choose.1), channel_id=1, source_target_pairs={{0,8},{8,0},{16,24},{24,16},{32,40},{40,32},{48,56},{56,48},{64,72... | collective-permute-start | bytes 589832 | tf_op jit(solution)/shard_map/ppermute | solution.py:418
  46.3 0.5 %slice_bitcast_fusion = f32[64]{0:T(128)} fusion(f32[1,128]{1,0:T(1,128)S(1)} %get-tuple-element.39), kind=kLoop, calls=%fused_computation | loop fusion | bytes 512 | tf_op jit(solution)/shard_map/squeeze | solution.py:435
  46.8 0.0 collective-permute-done.9.rest_3_
  46.9 0.6 %update_rows.1.part_ref = f32[1088,512]{1,0:T(8,128)S(1)} custom-call(f32[1088,512]{1,0:T(8,128)S(1)} %bitcast.6, bf16[1088,128]{1,0:T(8,128)(2,1)S(1)} %get-tuple-element.23.hot_ref.hot_cols_ref, f32[2,48,128]{2,1,0:T(8,128)S(1)} %pair.1.rest_0_, f32[2,48,128]{2,1,0:T(8,128)S(1)} %collective-permute-done.7.rest_1_, ...), custom_call_target="tpu_custom_call" | custom-call | tf_op jit(solution)/shard_map/update_rows/pallas_call | solution.py:421
  47.5 0.0 collective-permute-done.10.core_ref
  47.5 1.7 %update_cols.1 = f32[1088,512]{1,0:T(8,128)} custom-call(f32[1088,512]{1,0:T(8,128)S(1)} %update_rows.1.part_ref, f32[8,48,128]{2,1,0:T(8,128)S(1)} %all-to-all-done.1.z_ref, f32[48,128]{1,0:T(8,128)S(1)} %get-tuple-element.38.other_ref, f32[8,48,128]{2,1,0:T(8,128)S(1)} %collective-permute-done.10.core_ref, bf16[128,512]{1,0:T(8,128)(2,1)S(1)} %get-tuple-element.28.hot_rows_ref), custom_call_target="tpu_custom_call" | custom-call | tf_op jit(solution)/shard_map/update_cols/pallas_call | solution.py:424
  (9 shorter events, 0.1 us)
Async XLA Ops:
  4.6 4.4 %collective-permute-start = (f32[8,48,128]{2,1,0:T(8,128)S(1)}, f32[8,48,128]{2,1,0:T(8,128)S(1)}, u32[]{:S(2)}, u32[]{:S(2)}) collective-permute-start(f32[8,48,128]{2,1,0:T(8,128)S(1)} %get-tuple-element.25), channel_id=1, source_target_pairs={{0,8},{8,0},{16,24},{24,16},{32,40},{40,32},{48,56},{56,48},{64,72... | collective-permute-start | bytes 589832 | tf_op jit(solution)/shard_map/ppermute | solution.py:394
  7.9 10.4 %collective-permute-start.1 = (f32[4,48,128]{2,1,0:T(8,128)S(1)}, f32[4,48,128]{2,1,0:T(8,128)S(1)}, u32[]{:S(2)}, u32[]{:S(2)}) collective-permute-start(f32[4,48,128]{2,1,0:T(8,128)S(1)} %get-tuple-element.30), channel_id=1, source_target_pairs={{0,4},{1,5},{2,6},{3,7},{4,0},{5,1},{6,2},{7,3},{8,12},{9,13},{10,... | collective-permute-start | bytes 294920 | tf_op jit(solution)/shard_map/ppermute | solution.py:39
  9.7 15.7 %all-to-all-start = ((f32[8,48,128]{2,1,0:T(8,128)}), f32[8,48,128]{2,1,0:T(8,128)S(1)}, u32[]{:S(2)}, u32[]{:S(2)}) async-start(f32[8,48,128]{2,1,0:T(8,128)} %get-tuple-element.26), calls=%async_computation | async-start | bytes 393216 | tf_op jit(solution)/shard_map/all_to_all | solution.py:31
  18.4 11.6 %copy-start.1 = (f32[16384]{0:T(1024)S(1)}, f32[16384]{0:T(1024)}, u32[]{:S(2)}) copy-start(f32[16384]{0:T(1024)} %param.4) | copy-start | bytes 196612
  18.4 4.3 %collective-permute-start.2 = (f32[48,128]{1,0:T(8,128)S(1)}, f32[48,128]{1,0:T(8,128)S(1)}, u32[]{:S(2)}, u32[]{:S(2)}) collective-permute-start(f32[48,128]{1,0:T(8,128)S(1)} %get-tuple-element.31), channel_id=1, source_target_pairs={{0,3},{1,2},{2,1},{3,0},{4,7},{5,6},{6,5},{7,4},{8,11},{9,10},{10,... | collective-permute-start | bytes 73736 | tf_op jit(solution)/shard_map/ppermute | solution.py:39
  21.2 4.2 %collective-permute-start.3 = (f32[48,128]{1,0:T(8,128)S(1)}, f32[48,128]{1,0:T(8,128)S(1)}, u32[]{:S(2)}, u32[]{:S(2)}) collective-permute-start(f32[48,128]{1,0:T(8,128)S(1)} %get-tuple-element.32), channel_id=1, source_target_pairs={{0,2},{1,3},{2,0},{3,1},{4,6},{5,7},{6,4},{7,5},{8,10},{9,11},{10,... | collective-permute-start | bytes 73736 | tf_op jit(solution)/shard_map/ppermute | solution.py:39
  21.6 3.8 %collective-permute-start.4 = (f32[48,128]{1,0:T(8,128)S(1)}, f32[48,128]{1,0:T(8,128)S(1)}, u32[]{:S(2)}, u32[]{:S(2)}) collective-permute-start(f32[48,128]{1,0:T(8,128)S(1)} %get-tuple-element.33), channel_id=1, source_target_pairs={{0,1},{1,0},{2,3},{3,2},{4,5},{5,4},{6,7},{7,6},{8,9},{9,8},{10,11... | collective-permute-start | bytes 73736 | tf_op jit(solution)/shard_map/ppermute | solution.py:39
  25.5 4.5 %collective-permute-start.5 = (f32[96,128]{1,0:T(8,128)S(1)}, f32[96,128]{1,0:T(8,128)S(1)}, u32[]{:S(2)}, u32[]{:S(2)}) collective-permute-start(f32[96,128]{1,0:T(8,128)S(1)} %sum_parts.1.here_ref), channel_id=1, source_target_pairs={{0,128},{8,136},{16,144},{24,152},{32,160},{40,168},{48,176},{56,1... | collective-permute-start | bytes 147464 | tf_op jit(solution)/shard_map/ppermute | solution.py:408
  30.8 5.6 %collective-permute-start.6 = (f32[48,128]{1,0:T(8,128)S(1)}, f32[48,128]{1,0:T(8,128)S(1)}, u32[]{:S(2)}, u32[]{:S(2)}) collective-permute-start(f32[48,128]{1,0:T(8,128)S(1)} %get-tuple-element.36.own_ref), channel_id=1, source_target_pairs={{0,4},{1,5},{2,6},{3,7},{4,0},{5,1},{6,2},{7,3},{8,12},{9,13},{10,... | collective-permute-start | bytes 73736 | tf_op jit(solution)/shard_map/ppermute | solution.py:39
  31.9 9.9 %all-to-all-start.1 = ((f32[8,48,128]{2,1,0:T(8,128)}), f32[8,48,128]{2,1,0:T(8,128)S(1)}, u32[]{:S(2)}, u32[]{:S(2)}) async-start(f32[8,48,128]{2,1,0:T(8,128)} %get-tuple-element.37), calls=%async_computation.1 | async-start | bytes 393216 | tf_op jit(solution)/shard_map/all_to_all | solution.py:31
  36.4 10.4 %copy-start = (f32[512,1088]{0,1:T(8,128)S(1)}, f32[512,1088]{0,1:T(8,128)}, u32[]{:S(2)}) copy-start(f32[512,1088]{0,1:T(8,128)} %param.5) | copy-start | bytes 6684676
  36.5 10.4 %collective-permute-start.9 = (f32[2,48,128]{2,1,0:T(8,128)S(1)}, f32[2,48,128]{2,1,0:T(8,128)S(1)}, u32[]{:S(2)}, u32[]{:S(2)}) collective-permute-start(f32[2,48,128]{2,1,0:T(8,128)S(1)} %pair.1.rest_0_), channel_id=1, source_target_pairs={{0,3},{1,2},{2,1},{3,0},{4,7},{5,6},{6,5},{7,4},{8,11},{9,10},{10,... | collective-permute-start | bytes 147464 | tf_op jit(solution)/shard_map/ppermute | solution.py:39
  39.3 7.6 %collective-permute-start.8 = (f32[2,48,128]{2,1,0:T(8,128)S(1)}, f32[2,48,128]{2,1,0:T(8,128)S(1)}, u32[]{:S(2)}, u32[]{:S(2)}) collective-permute-start(f32[2,48,128]{2,1,0:T(8,128)S(1)} %pair.1.rest_0_), channel_id=1, source_target_pairs={{0,2},{1,3},{2,0},{3,1},{4,6},{5,7},{6,4},{7,5},{8,10},{9,11},{10,... | collective-permute-start | bytes 147464 | tf_op jit(solution)/shard_map/ppermute | solution.py:39
  39.6 7.2 %collective-permute-start.7 = (f32[2,48,128]{2,1,0:T(8,128)S(1)}, f32[2,48,128]{2,1,0:T(8,128)S(1)}, u32[]{:S(2)}, u32[]{:S(2)}) collective-permute-start(f32[2,48,128]{2,1,0:T(8,128)S(1)} %pair.1.rest_0_), channel_id=1, source_target_pairs={{0,1},{1,0},{2,3},{3,2},{4,5},{5,4},{6,7},{7,6},{8,9},{9,8},{10,11... | collective-permute-start | bytes 147464 | tf_op jit(solution)/shard_map/ppermute | solution.py:39
  41.8 5.7 %collective-permute-start.10 = (f32[8,48,128]{2,1,0:T(8,128)S(1)}, f32[8,48,128]{2,1,0:T(8,128)S(1)}, u32[]{:S(2)}, u32[]{:S(2)}) collective-permute-start(f32[8,48,128]{2,1,0:T(8,128)S(1)} %choose.1), channel_id=1, source_target_pairs={{0,8},{8,0},{16,24},{24,16},{32,40},{40,32},{48,56},{56,48},{64,72... | collective-permute-start | bytes 589832 | tf_op jit(solution)/shard_map/ppermute | solution.py:418

commit v6 on v5

--- a/solution.py
+++ b/solution.py
@@ -123,10 +123,9 @@
             codes = jnp.where((lane < PIECE) & jnp.logical_not(dead), codes, -1.0)
         hot[:, pair * 128 : pair * 128 + 128] = (codes == state).astype(f32).astype(bf16)
     part = None
-    for chunk, at in enumerate(CHUNKS):
-        if chunk % 2 == 0:
-            band_copies[chunk].wait()
-            band_copies[chunk + 1].wait()
+    for copy in band_copies:
+        copy.wait()
+    for at in CHUNKS:
         hi, lo = split(band[at, :])
         col_t[at, :] = mm(hi, hot_rows) + mm(lo, hot_rows)
         term = mm(hot[:, at], hi) + mm(hot[:, at], lo)

time: 49.4 us -> 49.2 us (level)
  no operation moved by 1% of the time
where the time goes in v6:
time: 49.2 us; the launch traced here: 48.9 us
  starting transfers between devices  31.8 us (65%)
  Pallas kernels  7.96 us (16%)
  waiting for transfers between devices  7.89 us (16%)
  between operations  0.72 us (1%)
  local copies, waits for them, and re-layouts  0.52 us (1%)
    all_to_all x2, starting transfers between devices, z_exchange(): return lax.all_to_all(x, 'row', 0, 0, tiled=True, axis_index_groups=groups)  13.2 us
    ppermute x8, starting transfers between devices, swap_cols(): return lax.ppermute(x, 'col', [(i, i ^ step) for i in range(COLS)])  8.05 us
    ppermute x1, starting transfers between devices, shards(): lax.ppermute(call(choose_kernel, eight, name='choose')(z_all, other), 'ro...  4.57 us
    pallas_call x1, Pallas kernels, shards(): call(logits_kernel, (arr(2, LOCI, BATCH), eight, eight, four, four, arr(B...  3.74 us
    ppermute x1, starting transfers between devices, shards(): core = lax.ppermute(core, 'row', SWAP_CORES)  3.33 us
    ppermute x8, waiting for transfers between devices, swap_cols(): return lax.ppermute(x, 'col', [(i, i ^ step) for i in range(COLS)])  3.18 us
    ppermute x1, starting transfers between devices, shards(): there = lax.ppermute(here, 'row', SWAP_HALVES)  2.66 us
    ppermute x1, waiting for transfers between devices, shards(): there = lax.ppermute(here, 'row', SWAP_HALVES)  1.87 us
  transfers between devices with their start and end apart: 13, of which 5 were waited for; matrix products, arithmetic and copies ran while one was open for 1% of the time, Pallas kernels for 3%

profile of v6, /device:TPU:1, one launch (start us, length us, event | category | flops | bytes accessed | tf_op | source)
XLA Modules:
  0.0 48.9 jit_solution(3656502617578554137)
XLA Ops:
  0.6 3.7 %logit_parts.1 = (f32[2,16,128]{2,1,0:T(8,128)S(1)}, f32[8,48,128]{2,1,0:T(8,128)S(1)}, f32[8,48,128]{2,1,0:T(8,128)S(1)}, f32[4,48,128]{2,1,0:T(8,128)S(1)}, f3...) custom-call(s32[128,4096]{1,0:T(8,128)} %seqs_ref.1, f32[1088,512]{1,0:T(8,128)} %bitcast.5), custom_call_target="tpu_custom_call" | custom-call | tf_op jit(solution)/shard_map/logit_parts/pallas_call | solution.py:371
  4.4 3.3 %collective-permute-start = (f32[8,48,128]{2,1,0:T(8,128)S(1)}, f32[8,48,128]{2,1,0:T(8,128)S(1)}, u32[]{:S(2)}, u32[]{:S(2)}) collective-permute-start(f32[8,48,128]{2,1,0:T(8,128)S(1)} %get-tuple-element.25), channel_id=1, source_target_pairs={{0,8},{8,0},{16,24},{24,16},{32,40},{40,32},{48,56},{56,48},{64,72... | collective-permute-start | bytes 589832 | tf_op jit(solution)/shard_map/ppermute | solution.py:393
  7.7 0.0 collective-permute-start.1
  7.7 1.1 %collective-permute-done.core_ref = f32[8,48,128]{2,1,0:T(8,128)S(1)} collective-permute-done((f32[8,48,128]{2,1,0:T(8,128)S(1)}, f32[8,48,128]{2,1,0:T(8,128)S(1)}, u32[]{:S(2)}, u32[]{:S(2)}) %collective-permute-start) | collective-permute-done | bytes 196640 | tf_op jit(solution)/shard_map/ppermute | solution.py:393
  8.8 0.7 %combine.1 = (f32[8,48,128]{2,1,0:T(8,128)}, f32[48,128]{1,0:T(8,128)S(1)}) custom-call(f32[8,48,128]{2,1,0:T(8,128)S(1)} %get-tuple-element.24.mine_ref, f32[8,48,128]{2,1,0:T(8,128)S(1)} %collective-permute-done.core_ref), custom_call_target="tpu_custom_call" | custom-call | tf_op jit(solution)/shard_map/combine/pallas_call | solution.py:395
  9.5 8.7 %all-to-all-start = ((f32[8,48,128]{2,1,0:T(8,128)}), f32[8,48,128]{2,1,0:T(8,128)S(1)}, u32[]{:S(2)}, u32[]{:S(2)}) async-start(f32[8,48,128]{2,1,0:T(8,128)} %get-tuple-element.26), calls=%async_computation | async-start | bytes 393216 | tf_op jit(solution)/shard_map/all_to_all | solution.py:31
  18.2 2.8 %collective-permute-start.2 = (f32[48,128]{1,0:T(8,128)S(1)}, f32[48,128]{1,0:T(8,128)S(1)}, u32[]{:S(2)}, u32[]{:S(2)}) collective-permute-start(f32[48,128]{1,0:T(8,128)S(1)} %get-tuple-element.31), channel_id=1, source_target_pairs={{0,3},{1,2},{2,1},{3,0},{4,7},{5,6},{6,5},{7,4},{8,11},{9,10},{10,... | collective-permute-start | bytes 73736 | tf_op jit(solution)/shard_map/ppermute | solution.py:39
  21.0 0.3 collective-permute-start.3
  21.3 0.3 collective-permute-start.4
  21.7 0.3 flip.1
  22.0 0.5 %collective-permute-done.2.rest_0_ = f32[48,128]{1,0:T(8,128)S(1)} collective-permute-done((f32[48,128]{1,0:T(8,128)S(1)}, f32[48,128]{1,0:T(8,128)S(1)}, u32[]{:S(2)}, u32[]{:S(2)}) %collective-permute-start.2) | collective-permute-done | bytes 24608 | tf_op jit(solution)/shard_map/ppermute | solution.py:39
  22.5 2.7 %collective-permute-done.3.rest_1_ = f32[48,128]{1,0:T(8,128)S(1)} collective-permute-done((f32[48,128]{1,0:T(8,128)S(1)}, f32[48,128]{1,0:T(8,128)S(1)}, u32[]{:S(2)}, u32[]{:S(2)}) %collective-permute-start.3) | collective-permute-done | bytes 24608 | tf_op jit(solution)/shard_map/ppermute | solution.py:39
  25.2 0.0 all-to-all-done.z_ref
  25.2 0.1 sum_parts.1.here_ref
  25.2 2.7 %collective-permute-start.5 = (f32[96,128]{1,0:T(8,128)S(1)}, f32[96,128]{1,0:T(8,128)S(1)}, u32[]{:S(2)}, u32[]{:S(2)}) collective-permute-start(f32[96,128]{1,0:T(8,128)S(1)} %sum_parts.1.here_ref), channel_id=1, source_target_pairs={{0,128},{8,136},{16,144},{24,152},{32,160},{40,168},{48,176},{56,1... | collective-permute-start | bytes 147464 | tf_op jit(solution)/shard_map/ppermute | solution.py:407
  27.9 1.9 %collective-permute-done.5.there_ref = f32[96,128]{1,0:T(8,128)S(1)} collective-permute-done((f32[96,128]{1,0:T(8,128)S(1)}, f32[96,128]{1,0:T(8,128)S(1)}, u32[]{:S(2)}, u32[]{:S(2)}) %collective-permute-start.5) | collective-permute-done | bytes 49184 | tf_op jit(solution)/shard_map/ppermute | solution.py:407
  29.8 0.8 %softmax.1 = (f32[8,48,128]{2,1,0:T(8,128)}, f32[48,128]{1,0:T(8,128)S(1)}, f32[48,128]{1,0:T(8,128)S(1)}, f32[1,128]{1,0:T(1,128)S(1)}) custom-call(f32[96,128]{1,0:T(8,128)S(1)} %sum_parts.1.here_ref, f32[96,128]{1,0:T(8,128)S(1)} %collective-permute-done.5.there_ref, f32[2,16,128]{2,1,0:T(8,128)S(1)} %get-tuple-element.35.codes_ref, f32[128,128]{1,0:T(8,128)S(1)} %bitcast.7), custom_call_target="tpu_custom_call" | custom-call | tf_op jit(solution)/shard_map/softmax/pallas_call | solution.py:408
  30.6 1.0 %collective-permute-start.6 = (f32[48,128]{1,0:T(8,128)S(1)}, f32[48,128]{1,0:T(8,128)S(1)}, u32[]{:S(2)}, u32[]{:S(2)}) collective-permute-start(f32[48,128]{1,0:T(8,128)S(1)} %get-tuple-element.36.own_ref), channel_id=1, source_target_pairs={{0,4},{1,5},{2,6},{3,7},{4,0},{5,1},{6,2},{7,3},{8,12},{9,13},{10,... | collective-permute-start | bytes 73736 | tf_op jit(solution)/shard_map/ppermute | solution.py:39
  31.6 4.6 %all-to-all-start.1 = ((f32[8,48,128]{2,1,0:T(8,128)}), f32[8,48,128]{2,1,0:T(8,128)S(1)}, u32[]{:S(2)}, u32[]{:S(2)}) async-start(f32[8,48,128]{2,1,0:T(8,128)} %get-tuple-element.37), calls=%async_computation.1 | async-start | bytes 393216 | tf_op jit(solution)/shard_map/all_to_all | solution.py:31
  36.2 0.0 collective-permute-done.6.got_ref
  36.2 2.8 %collective-permute-start.9 = (f32[2,48,128]{2,1,0:T(8,128)S(1)}, f32[2,48,128]{2,1,0:T(8,128)S(1)}, u32[]{:S(2)}, u32[]{:S(2)}) collective-permute-start(f32[2,48,128]{2,1,0:T(8,128)S(1)} %pair.1.rest_0_), channel_id=1, source_target_pairs={{0,3},{1,2},{2,1},{3,0},{4,7},{5,6},{6,5},{7,4},{8,11},{9,10},{10,... | collective-permute-start | bytes 147464 | tf_op jit(solution)/shard_map/ppermute | solution.py:39
  39.1 0.3 collective-permute-start.8
  39.4 0.3 collective-permute-start.7
  39.7 1.8 %all-to-all-done.1.z_ref = f32[8,48,128]{2,1,0:T(8,128)S(1)} async-done(((f32[8,48,128]{2,1,0:T(8,128)}), f32[8,48,128]{2,1,0:T(8,128)S(1)}, u32[]{:S(2)}, u32[]{:S(2)}) %all-to-all-start.1) | async-done | bytes 196640 | tf_op jit(solution)/shard_map/all_to_all | solution.py:31
  41.5 4.6 %collective-permute-start.10 = (f32[8,48,128]{2,1,0:T(8,128)S(1)}, f32[8,48,128]{2,1,0:T(8,128)S(1)}, u32[]{:S(2)}, u32[]{:S(2)}) collective-permute-start(f32[8,48,128]{2,1,0:T(8,128)S(1)} %choose.1), channel_id=1, source_target_pairs={{0,8},{8,0},{16,24},{24,16},{32,40},{40,32},{48,56},{56,48},{64,72... | collective-permute-start | bytes 589832 | tf_op jit(solution)/shard_map/ppermute | solution.py:417
  46.1 0.5 %slice_bitcast_fusion = f32[64]{0:T(128)} fusion(f32[1,128]{1,0:T(1,128)S(1)} %get-tuple-element.39), kind=kLoop, calls=%fused_computation | loop fusion | bytes 512 | tf_op jit(solution)/shard_map/squeeze | solution.py:434
  46.6 0.0 collective-permute-done.9.rest_3_
  46.6 0.0 collective-permute-done.8.rest_2_
  46.6 0.0 collective-permute-done.7.rest_1_
  46.6 0.6 %update_rows.1.part_ref = f32[1088,512]{1,0:T(8,128)S(1)} custom-call(f32[1088,512]{1,0:T(8,128)S(1)} %bitcast.6, bf16[1088,128]{1,0:T(8,128)(2,1)S(1)} %get-tuple-element.23.hot_ref.hot_cols_ref, f32[2,48,128]{2,1,0:T(8,128)S(1)} %pair.1.rest_0_, f32[2,48,128]{2,1,0:T(8,128)S(1)} %collective-permute-done.7.rest_1_, ...), custom_call_target="tpu_custom_call" | custom-call | tf_op jit(solution)/shard_map/update_rows/pallas_call | solution.py:420
  47.3 0.0 collective-permute-done.10.core_ref
  47.3 1.7 %update_cols.1 = f32[1088,512]{1,0:T(8,128)} custom-call(f32[1088,512]{1,0:T(8,128)S(1)} %update_rows.1.part_ref, f32[8,48,128]{2,1,0:T(8,128)S(1)} %all-to-all-done.1.z_ref, f32[48,128]{1,0:T(8,128)S(1)} %get-tuple-element.38.other_ref, f32[8,48,128]{2,1,0:T(8,128)S(1)} %collective-permute-done.10.core_ref, bf16[128,512]{1,0:T(8,128)(2,1)S(1)} %get-tuple-element.28.hot_rows_ref), custom_call_target="tpu_custom_call" | custom-call | tf_op jit(solution)/shard_map/update_cols/pallas_call | solution.py:423
  (9 shorter events, 0.1 us)
Async XLA Ops:
  4.4 4.4 %collective-permute-start = (f32[8,48,128]{2,1,0:T(8,128)S(1)}, f32[8,48,128]{2,1,0:T(8,128)S(1)}, u32[]{:S(2)}, u32[]{:S(2)}) collective-permute-start(f32[8,48,128]{2,1,0:T(8,128)S(1)} %get-tuple-element.25), channel_id=1, source_target_pairs={{0,8},{8,0},{16,24},{24,16},{32,40},{40,32},{48,56},{56,48},{64,72... | collective-permute-start | bytes 589832 | tf_op jit(solution)/shard_map/ppermute | solution.py:393
  7.7 10.4 %collective-permute-start.1 = (f32[4,48,128]{2,1,0:T(8,128)S(1)}, f32[4,48,128]{2,1,0:T(8,128)S(1)}, u32[]{:S(2)}, u32[]{:S(2)}) collective-permute-start(f32[4,48,128]{2,1,0:T(8,128)S(1)} %get-tuple-element.30), channel_id=1, source_target_pairs={{0,4},{1,5},{2,6},{3,7},{4,0},{5,1},{6,2},{7,3},{8,12},{9,13},{10,... | collective-permute-start | bytes 294920 | tf_op jit(solution)/shard_map/ppermute | solution.py:39
  9.5 15.7 %all-to-all-start = ((f32[8,48,128]{2,1,0:T(8,128)}), f32[8,48,128]{2,1,0:T(8,128)S(1)}, u32[]{:S(2)}, u32[]{:S(2)}) async-start(f32[8,48,128]{2,1,0:T(8,128)} %get-tuple-element.26), calls=%async_computation | async-start | bytes 393216 | tf_op jit(solution)/shard_map/all_to_all | solution.py:31
  18.1 11.6 %copy-start.1 = (f32[16384]{0:T(1024)S(1)}, f32[16384]{0:T(1024)}, u32[]{:S(2)}) copy-start(f32[16384]{0:T(1024)} %param.4) | copy-start | bytes 196612
  18.2 4.3 %collective-permute-start.2 = (f32[48,128]{1,0:T(8,128)S(1)}, f32[48,128]{1,0:T(8,128)S(1)}, u32[]{:S(2)}, u32[]{:S(2)}) collective-permute-start(f32[48,128]{1,0:T(8,128)S(1)} %get-tuple-element.31), channel_id=1, source_target_pairs={{0,3},{1,2},{2,1},{3,0},{4,7},{5,6},{6,5},{7,4},{8,11},{9,10},{10,... | collective-permute-start | bytes 73736 | tf_op jit(solution)/shard_map/ppermute | solution.py:39
  21.0 4.2 %collective-permute-start.3 = (f32[48,128]{1,0:T(8,128)S(1)}, f32[48,128]{1,0:T(8,128)S(1)}, u32[]{:S(2)}, u32[]{:S(2)}) collective-permute-start(f32[48,128]{1,0:T(8,128)S(1)} %get-tuple-element.32), channel_id=1, source_target_pairs={{0,2},{1,3},{2,0},{3,1},{4,6},{5,7},{6,4},{7,5},{8,10},{9,11},{10,... | collective-permute-start | bytes 73736 | tf_op jit(solution)/shard_map/ppermute | solution.py:39
  21.3 3.8 %collective-permute-start.4 = (f32[48,128]{1,0:T(8,128)S(1)}, f32[48,128]{1,0:T(8,128)S(1)}, u32[]{:S(2)}, u32[]{:S(2)}) collective-permute-start(f32[48,128]{1,0:T(8,128)S(1)} %get-tuple-element.33), channel_id=1, source_target_pairs={{0,1},{1,0},{2,3},{3,2},{4,5},{5,4},{6,7},{7,6},{8,9},{9,8},{10,11... | collective-permute-start | bytes 73736 | tf_op jit(solution)/shard_map/ppermute | solution.py:39
  25.2 4.5 %collective-permute-start.5 = (f32[96,128]{1,0:T(8,128)S(1)}, f32[96,128]{1,0:T(8,128)S(1)}, u32[]{:S(2)}, u32[]{:S(2)}) collective-permute-start(f32[96,128]{1,0:T(8,128)S(1)} %sum_parts.1.here_ref), channel_id=1, source_target_pairs={{0,128},{8,136},{16,144},{24,152},{32,160},{40,168},{48,176},{56,1... | collective-permute-start | bytes 147464 | tf_op jit(solution)/shard_map/ppermute | solution.py:407
  30.6 5.6 %collective-permute-start.6 = (f32[48,128]{1,0:T(8,128)S(1)}, f32[48,128]{1,0:T(8,128)S(1)}, u32[]{:S(2)}, u32[]{:S(2)}) collective-permute-start(f32[48,128]{1,0:T(8,128)S(1)} %get-tuple-element.36.own_ref), channel_id=1, source_target_pairs={{0,4},{1,5},{2,6},{3,7},{4,0},{5,1},{6,2},{7,3},{8,12},{9,13},{10,... | collective-permute-start | bytes 73736 | tf_op jit(solution)/shard_map/ppermute | solution.py:39
  31.6 9.9 %all-to-all-start.1 = ((f32[8,48,128]{2,1,0:T(8,128)}), f32[8,48,128]{2,1,0:T(8,128)S(1)}, u32[]{:S(2)}, u32[]{:S(2)}) async-start(f32[8,48,128]{2,1,0:T(8,128)} %get-tuple-element.37), calls=%async_computation.1 | async-start | bytes 393216 | tf_op jit(solution)/shard_map/all_to_all | solution.py:31
  36.2 10.4 %copy-start = (f32[512,1088]{0,1:T(8,128)S(1)}, f32[512,1088]{0,1:T(8,128)}, u32[]{:S(2)}) copy-start(f32[512,1088]{0,1:T(8,128)} %param.5) | copy-start | bytes 6684676
  36.2 10.4 %collective-permute-start.9 = (f32[2,48,128]{2,1,0:T(8,128)S(1)}, f32[2,48,128]{2,1,0:T(8,128)S(1)}, u32[]{:S(2)}, u32[]{:S(2)}) collective-permute-start(f32[2,48,128]{2,1,0:T(8,128)S(1)} %pair.1.rest_0_), channel_id=1, source_target_pairs={{0,3},{1,2},{2,1},{3,0},{4,7},{5,6},{6,5},{7,4},{8,11},{9,10},{10,... | collective-permute-start | bytes 147464 | tf_op jit(solution)/shard_map/ppermute | solution.py:39
  39.1 7.6 %collective-permute-start.8 = (f32[2,48,128]{2,1,0:T(8,128)S(1)}, f32[2,48,128]{2,1,0:T(8,128)S(1)}, u32[]{:S(2)}, u32[]{:S(2)}) collective-permute-start(f32[2,48,128]{2,1,0:T(8,128)S(1)} %pair.1.rest_0_), channel_id=1, source_target_pairs={{0,2},{1,3},{2,0},{3,1},{4,6},{5,7},{6,4},{7,5},{8,10},{9,11},{10,... | collective-permute-start | bytes 147464 | tf_op jit(solution)/shard_map/ppermute | solution.py:39
  39.4 7.2 %collective-permute-start.7 = (f32[2,48,128]{2,1,0:T(8,128)S(1)}, f32[2,48,128]{2,1,0:T(8,128)S(1)}, u32[]{:S(2)}, u32[]{:S(2)}) collective-permute-start(f32[2,48,128]{2,1,0:T(8,128)S(1)} %pair.1.rest_0_), channel_id=1, source_target_pairs={{0,1},{1,0},{2,3},{3,2},{4,5},{5,4},{6,7},{7,6},{8,9},{9,8},{10,11... | collective-permute-start | bytes 147464 | tf_op jit(solution)/shard_map/ppermute | solution.py:39
  41.5 5.7 %collective-permute-start.10 = (f32[8,48,128]{2,1,0:T(8,128)S(1)}, f32[8,48,128]{2,1,0:T(8,128)S(1)}, u32[]{:S(2)}, u32[]{:S(2)}) collective-permute-start(f32[8,48,128]{2,1,0:T(8,128)S(1)} %choose.1), channel_id=1, source_target_pairs={{0,8},{8,0},{16,24},{24,16},{32,40},{40,32},{48,56},{56,48},{64,72... | collective-permute-start | bytes 589832 | tf_op jit(solution)/shard_map/ppermute | solution.py:417
